TPU v7x, 32 devices: a whole 2x2x4 slice. The times are simulated.
32 devices in a mesh: row: 4 (over z), col: 8 (over y, x, core).
Axes of the slice: x: 2, y: 2, z: 4, core: 2. Of those that a mesh axis runs over, the one named last changes fastest.
Arguments:
- tokens: bfloat16 [1024, 8192], P('row', 'col'), may hold values from -6 to 6
- cotangent: bfloat16 [1024, 8192], P('row', 'col'), may hold values from -6 to 6
- gate_weight: bfloat16 [8192, 14336], P('row', 'col'), may hold values from -0.1875 to 0.1875
- up_weight: bfloat16 [8192, 14336], P('row', 'col'), may hold values from -0.1875 to 0.1875
- down_weight: bfloat16 [14336, 8192], P('col', 'row'), may hold values from -0.125 to 0.125
- tile_mask: int32 [64, 112], replicated, may hold values from 0 to 1, as said below
Outputs:
- output: bfloat16 [1024, 8192], P('row', 'col')
- input_grad: bfloat16 [1024, 8192], P('row', 'col')
- gate_grad: bfloat16 [8192, 14336], P('row', 'col')
- up_grad: bfloat16 [8192, 14336], P('row', 'col')
- down_grad: bfloat16 [14336, 8192], P('col', 'row')
Inputs may be any that keep to these rules, and one draw needn't show every extreme that they name: `tile_mask`: the mask is made of 4 x 8 blocks of 16 x 14 tiles (block (i, j) holds tile rows i * 16.. and tile columns j * 14..). Each block holds between 8 and 48 ones, some block exactly 48, and the whole mask exactly 896 ones.
All inputs are finite; a program needn't handle non-finite values.
Results may differ from a plain program's by a relative error of at most 0.013.
Values may be sent and summed in bfloat16 or wider, within the bound.
A program may use at most 256 MiB of HBM per device.

v0:
```python
import jax
import jax.numpy as jnp
from jax import lax
from jax.sharding import PartitionSpec as P

BLK = 128


def on_device(tokens, cotangent, gate_weight, up_weight, down_weight, tile_mask):
    row_count = lax.axis_size("row")
    row_index = lax.axis_index("row")
    col_index = lax.axis_index("col")
    tok_rows = tokens.shape[0]
    block_rows, block_cols = gate_weight.shape
    row_tiles = block_rows // BLK
    col_tiles = block_cols // BLK
    tile_count = row_tiles * col_tiles
    mean_count = tile_count // 8
    capacity = mean_count + mean_count * 5 // 7
    all_row_tiles = row_tiles * row_count
    width = all_row_tiles * BLK
    column_mask = lax.dynamic_slice_in_dim(tile_mask, col_index * col_tiles, col_tiles, 1)
    grouped = column_mask.reshape(row_count, tile_count)
    places = jnp.arange(tile_count, dtype=jnp.int32)
    sort_keys = (1 - grouped) * tile_count + places[None, :]
    slot_order = jnp.argsort(sort_keys, axis=1)[:, :capacity]
    slot_valid = jnp.take_along_axis(grouped, slot_order, 1)
    offsets = (jnp.arange(row_count, dtype=jnp.int32) * row_tiles)[:, None]
    local_row = slot_order // col_tiles
    tile_row = (local_row + offsets).reshape(-1)
    tile_col = (slot_order % col_tiles).reshape(-1)
    valid_flat = slot_valid.reshape(-1).astype(jnp.float32)
    col_onehot = (tile_col[:, None] == jnp.arange(col_tiles, dtype=jnp.int32)[None, :]).astype(
        jnp.float32
    ) * valid_flat[:, None]
    group_onehot = (
        local_row[:, :, None] == jnp.arange(row_tiles, dtype=jnp.int32)[None, None, :]
    ).astype(jnp.float32) * slot_valid.astype(jnp.float32)[:, :, None]
    own_order = lax.dynamic_index_in_dim(slot_order, row_index, 0, keepdims=False)
    own_valid = lax.dynamic_index_in_dim(slot_valid, row_index, 0, keepdims=False).astype(
        jnp.bfloat16
    )
    highest = lax.Precision.HIGHEST

    def pack_in(weight):
        tiled = jnp.transpose(weight.reshape(row_tiles, BLK, col_tiles, BLK), (0, 2, 1, 3)).reshape(
            tile_count, BLK, BLK
        )
        return jnp.take(tiled, own_order, axis=0) * own_valid[:, None, None]

    def sum_cols(parts):
        return jnp.einsum("tsn,sj->tjn", parts, col_onehot, precision=highest).reshape(
            tok_rows, block_cols
        )

    def sum_rows(parts):
        blocked = parts.reshape(tok_rows, row_count, capacity, BLK)
        return jnp.einsum("tgcn,gcr->tgrn", blocked, group_onehot, precision=highest).reshape(
            tok_rows, width
        )

    packed_gate = pack_in(gate_weight)
    packed_up = pack_in(up_weight)
    tiled = jnp.transpose(
        down_weight.reshape(col_tiles, BLK, row_tiles, BLK), (2, 0, 1, 3)
    ).reshape(tile_count, BLK, BLK)
    packed_down = jnp.take(tiled, own_order, axis=0) * own_valid[:, None, None]
    gathered_tokens = lax.all_gather(tokens, "col", axis=1, tiled=True)
    token_tiles = jnp.take(gathered_tokens.reshape(tok_rows, all_row_tiles, BLK), tile_row, axis=1)
    gate_tiles, up_tiles = (
        lax.all_gather(packed_gate, "row", axis=0, tiled=True),
        lax.all_gather(packed_up, "row", axis=0, tiled=True),
    )
    gate = sum_cols(
        jnp.einsum("tsk,skn->tsn", token_tiles, gate_tiles, preferred_element_type=jnp.float32)
    )
    upper = sum_cols(
        jnp.einsum("tsk,skn->tsn", token_tiles, up_tiles, preferred_element_type=jnp.float32)
    )
    hidden = (jax.nn.silu(gate) * upper).astype(jnp.bfloat16)
    down_tiles = lax.all_gather(packed_down, "row", axis=0, tiled=True)
    hidden_tiles = jnp.take(hidden.reshape(tok_rows, col_tiles, BLK), tile_col, axis=1)
    out_terms = sum_rows(
        jnp.einsum("tsf,sfd->tsd", hidden_tiles, down_tiles, preferred_element_type=jnp.float32)
    )
    output = lax.psum_scatter(
        out_terms.astype(jnp.bfloat16), "col", scatter_dimension=1, tiled=True
    )
    gate_back_w, up_back_w = (gate_tiles, up_tiles)
    gathered_cot = lax.all_gather(cotangent, "col", axis=1, tiled=True)
    cot_tiles = jnp.take(gathered_cot.reshape(tok_rows, all_row_tiles, BLK), tile_row, axis=1)
    hidden_grad = sum_cols(
        jnp.einsum("tsd,sfd->tsf", cot_tiles, down_tiles, preferred_element_type=jnp.float32)
    )
    down_terms = (
        jnp.einsum("tsf,tsd->sfd", hidden_tiles, cot_tiles, preferred_element_type=jnp.float32)
        * valid_flat[:, None, None]
    )
    down_sums = lax.psum_scatter(
        down_terms.astype(jnp.bfloat16), "row", scatter_dimension=0, tiled=True
    )
    sigmoid_gate = jax.nn.sigmoid(gate)
    gate_cot = (hidden_grad * upper * sigmoid_gate * (1.0 + gate * (1.0 - sigmoid_gate))).astype(
        jnp.bfloat16
    )
    up_cot = (hidden_grad * jax.nn.silu(gate)).astype(jnp.bfloat16)
    gate_cot_tiles = jnp.take(gate_cot.reshape(tok_rows, col_tiles, BLK), tile_col, axis=1)
    up_cot_tiles = jnp.take(up_cot.reshape(tok_rows, col_tiles, BLK), tile_col, axis=1)
    gate_terms = (
        jnp.einsum("tsk,tsn->skn", token_tiles, gate_cot_tiles, preferred_element_type=jnp.float32)
        * valid_flat[:, None, None]
    )
    up_terms = (
        jnp.einsum("tsk,tsn->skn", token_tiles, up_cot_tiles, preferred_element_type=jnp.float32)
        * valid_flat[:, None, None]
    )
    gate_sums, up_sums = (
        lax.psum_scatter(
            gate_terms.astype(jnp.bfloat16), "row", scatter_dimension=0, tiled=True
        ).astype(jnp.float32),
        lax.psum_scatter(
            up_terms.astype(jnp.bfloat16), "row", scatter_dimension=0, tiled=True
        ).astype(jnp.float32),
    )
    input_terms = jnp.einsum(
        "tsn,skn->tsk", gate_cot_tiles, gate_back_w, preferred_element_type=jnp.float32
    )
    input_terms = input_terms + jnp.einsum(
        "tsn,skn->tsk", up_cot_tiles, up_back_w, preferred_element_type=jnp.float32
    )
    input_grad = lax.psum_scatter(
        sum_rows(input_terms).astype(jnp.bfloat16), "col", scatter_dimension=1, tiled=True
    )

    def unpack_in(summed):
        dense = (
            jnp.zeros((tile_count, BLK, BLK), jnp.bfloat16)
            .at[own_order]
            .set(summed.astype(jnp.bfloat16))
        )
        return jnp.transpose(dense.reshape(row_tiles, col_tiles, BLK, BLK), (0, 2, 1, 3)).reshape(
            block_rows, block_cols
        )

    dense = jnp.zeros((tile_count, BLK, BLK), jnp.bfloat16).at[own_order].set(down_sums)
    return (
        output,
        input_grad,
        unpack_in(gate_sums),
        unpack_in(up_sums),
        jnp.transpose(dense.reshape(row_tiles, col_tiles, BLK, BLK), (1, 2, 0, 3)).reshape(
            block_cols, block_rows
        ),
    )


def solution(mesh):
    return jax.shard_map(
        on_device,
        mesh=mesh,
        in_specs=(
            P("row", "col"),
            P("row", "col"),
            P("row", "col"),
            P("row", "col"),
            P("col", "row"),
            P(),
        ),
        out_specs=(
            P("row", "col"),
            P("row", "col"),
            P("row", "col"),
            P("row", "col"),
            P("col", "row"),
        ),
        check_vma=False,
    )
```

profile of v0, /device:TPU:0, one launch (start us, length us, event | category | flops | bytes accessed | tf_op | source)
XLA Modules:
  0.0 1106.3 jit_solution(18384377867712901926)
XLA Ops:
  7.2 2.0 copy.116
  9.3 2.0 copy.129
  11.7 3.3 sort.17
  17.2 9.0 copy.160
  26.2 4.5 bitcast_bitcast_fusion
  30.7 5.1 copy.113
  35.8 13.6 %reshape.316 = bf16[16,128,14,128]{3,2,1,0:T(8,128)(2,1)} reshape(bf16[2048,1792]{1,0:T(8,128)(2,1)} %param.15) | data formatting | bytes 14680064 | tf_op jit(solution)/shard_map/reshape | solution.py:46
  49.3 8.6 copy.122
  58.6 4.3 gather_fusion.1
  63.0 3.9 gather_fusion.4
  66.9 14.1 %reshape.315 = bf16[16,128,14,128]{3,2,1,0:T(8,128)(2,1)} reshape(bf16[2048,1792]{1,0:T(8,128)(2,1)} %param.14) | data formatting | bytes 14680064 | tf_op jit(solution)/shard_map/reshape | solution.py:46
  81.0 8.7 copy.115
  89.7 5.0 gather_fusion.2
  94.7 3.8 select_multiply_fusion.1
  100.7 6.4 copy.117
  107.0 6.6 copy.130
  113.6 10.5 gather_fusion.3
  124.1 10.5 gather_fusion.6
  134.5 82.2 %all-gather.12.cloned.1.call-done = bf16[192,128,128]{2,1,0:T(8,128)(2,1)} async-done(((bf16[48,128,128]{2,1,0:T(8,128)(2,1)}), bf16[192,128,128]{2,1,0:T(8,128)(2,1)}) %all-gather.12.cloned.1.call-update) | async-done | bytes 6291472 | tf_op jit(solution)/shard_map/all_gather | solution.py:72
  216.8 16.3 %fusion.24 = f32[256,192,128]{0,2,1:T(8,128)} fusion(bf16[192,128,128]{2,1,0:T(8,128)(2,1)} %all-gather.12.cloned.1.call-done, bf16[192,256,128]{2,1,0:T(8,128)(2,1)} %gather_fusion.3, pred[192]{0:T(512)(128)(4,1)S(1)} %get-tuple-element.47), kind=kOutput, calls=%fused_computation.42 | convolution fusion | flops 1616904192 | bytes 44040384 | tf_op jit(solution)/shard_map/tsk,skn->tsn/dot_general | solution.py:78
  233.1 24.8 %copy.124 = f32[256,192,128]{2,1,0:T(8,128)} copy(f32[256,192,128]{0,2,1:T(8,128)} %fusion.24) | data formatting | bytes 50331648 | tf_op jit(solution)/shard_map/tsk,skn->tsn/transpose | solution.py:78
  257.9 74.5 %all-gather.8.cloned.1.call-done = bf16[192,128,128]{2,1,0:T(8,128)(2,1)} async-done(((bf16[48,128,128]{2,1,0:T(8,128)(2,1)}), bf16[192,128,128]{2,1,0:T(8,128)(2,1)}) %all-gather.8.cloned.1.call-update) | async-done | bytes 6291472 | tf_op jit(solution)/shard_map/all_gather | solution.py:71
  332.4 16.3 %fusion.21 = f32[256,192,128]{0,2,1:T(8,128)} fusion(bf16[192,128,128]{2,1,0:T(8,128)(2,1)} %all-gather.8.cloned.1.call-done, bf16[192,256,128]{2,1,0:T(8,128)(2,1)} %gather_fusion.3, pred[192]{0:T(512)(128)(4,1)S(1)} %get-tuple-element.47), kind=kOutput, calls=%fused_computation.41 | convolution fusion | flops 1616904192 | bytes 44040384 | tf_op jit(solution)/shard_map/tsk,skn->tsn/dot_general | solution.py:75
  348.7 24.8 %copy.119 = f32[256,192,128]{2,1,0:T(8,128)} copy(f32[256,192,128]{0,2,1:T(8,128)} %fusion.21) | data formatting | bytes 50331648 | tf_op jit(solution)/shard_map/tsk,skn->tsn/transpose | solution.py:75
  373.6 17.0 %fusion.60 = f32[14,256,128]{2,0,1:T(8,128)} fusion(f32[256,192,128]{2,1,0:T(8,128)} %copy.124, f32[192]{0:T(256)S(1)} %convert_element_type.75, s32[192]{0:T(256)S(1)} %eq.33), kind=kOutput, calls=%fused_computation.76 | convolution fusion | flops 1056969984 | bytes 27002368 | tf_op jit(solution)/shard_map/tsn,sj->tjn/dot_general | solution.py:52
  390.5 13.2 %fusion.62 = f32[14,256,128]{2,0,1:T(8,128)} fusion(f32[256,192,128]{2,1,0:T(8,128)S(1)} %copy-done.2, f32[192]{0:T(256)S(1)} %convert_element_type.75, s32[192]{0:T(256)S(1)} %eq.33), kind=kOutput, calls=%fused_computation.78 | convolution fusion | flops 1056969984 | bytes 27002368 | tf_op jit(solution)/shard_map/tsn,sj->tjn/dot_general | solution.py:52
  403.7 43.7 %all-gather.6.cloned.1.call-done = bf16[192,128,128]{2,1,0:T(8,128)(2,1)} async-done(((bf16[48,128,128]{2,1,0:T(8,128)(2,1)}), bf16[192,128,128]{2,1,0:T(8,128)(2,1)}) %all-gather.6.cloned.1.call-update) | async-done | bytes 6291472 | tf_op jit(solution)/shard_map/all_gather | solution.py:81
  447.4 13.9 %fusion.27 = f32[256,192,128]{0,2,1:T(8,128)} fusion(bf16[192,128,128]{2,1,0:T(8,128)(2,1)} %all-gather.6.cloned.1.call-done, bf16[192,256,128]{2,1,0:T(8,128)(2,1)} %gather_fusion.6, pred[192]{0:T(512)(128)(4,1)S(1)} %get-tuple-element.47), kind=kOutput, calls=%fused_computation.43 | convolution fusion | flops 1616904192 | bytes 44040384 | tf_op jit(solution)/shard_map/tsd,sfd->tsf/dot_general | solution.py:93
  461.3 24.8 %copy.131 = f32[256,192,128]{2,1,0:T(8,128)} copy(f32[256,192,128]{0,2,1:T(8,128)} %fusion.27) | data formatting | bytes 50331648 | tf_op jit(solution)/shard_map/tsd,sfd->tsf/transpose | solution.py:93
  486.1 15.2 %fusion.58 = f32[14,256,128]{2,0,1:T(8,128)S(1)} fusion(f32[256,192,128]{2,1,0:T(8,128)} %copy.131, f32[192]{0:T(256)S(1)} %convert_element_type.75, s32[192]{0:T(256)S(1)} %eq.33), kind=kOutput, calls=%fused_computation.74 | convolution fusion | flops 1056969984 | bytes 27002368 | tf_op jit(solution)/shard_map/tsn,sj->tjn/dot_general | solution.py:52
  501.3 2.1 fusion.47
  503.4 8.2 gather_fusion.8
  511.6 8.0 gather_fusion.7
  519.6 13.8 %fusion.2 = f32[192,128,256]{2,1,0:T(8,128)} fusion(bf16[192,128,128]{2,1,0:T(8,128)(2,1)} %all-gather.12.cloned.1.call-done, bf16[192,256,128]{2,1,0:T(8,128)(2,1)} %gather_fusion.8, pred[192]{0:T(512)(128)(4,1)S(1)} %copy-done.11), kind=kOutput, calls=%fused_computation.14 | convolution fusion | flops 1616904192 | bytes 44040384 | tf_op jit(solution)/shard_map/tsn,skn->tsk/dot_general | solution.py:128
  533.4 24.3 %fusion.30 = f32[192,128,256]{2,1,0:T(8,128)} fusion(f32[192,128,256]{2,1,0:T(8,128)} %fusion.2, bf16[192,128,128]{2,1,0:T(8,128)(2,1)} %all-gather.8.cloned.1.call-done, bf16[192,256,128]{2,1,0:T(8,128)(2,1)} %gather_fusion.7, pred[192]{0:T(512)(128)(4,1)S(1)} %copy-done.11), kind=kOutput, calls=%fused_computation.48 | convolution fusion | flops 1623195648 | bytes 69206208 | tf_op jit(solution)/shard_map/tsn,skn->tsk/dot_general | solution.py:125
  557.8 24.8 %copy.133 = f32[256,4,48,128]{3,2,0,1:T(8,128)} copy(f32[256,4,48,128]{0,3,2,1:T(8,128)} %bitcast.183) | data formatting | bytes 50331648 | tf_op jit(solution)/shard_map/reshape | solution.py:57
  582.5 16.2 %convert_bitcast_fusion = bf16[256,4,16,128]{3,2,0,1:T(8,128)(2,1)} fusion(f32[256,4,48,128]{3,2,0,1:T(8,128)} %copy.133, f32[4,48]{1,0:T(4,128)S(1)} %copy-done.9, s32[4,48]{1,0:T(4,128)S(1)} %copy-done.10), kind=kOutput, calls=%fused_computation.49 | convolution fusion | flops 1210062848 | bytes 29361664 | tf_op jit(solution)/shard_map/tgcn,gcr->tgrn/dot_general | solution.py:58
  598.7 7.5 copy.134
  606.2 8.7 gather_fusion.5
  614.9 16.7 %fusion.13 = f32[192,128,256]{2,1,0:T(8,128)} fusion(bf16[192,128,128]{2,1,0:T(8,128)(2,1)} %all-gather.6.cloned.1.call-done, bf16[192,256,128]{2,1,0:T(8,128)(2,1)} %gather_fusion.5, pred[192]{0:T(512)(128)(4,1)S(1)} %copy-done.11), kind=kOutput, calls=%fused_computation.25 | convolution fusion | flops 1616904192 | bytes 44040384 | tf_op jit(solution)/shard_map/tsf,sfd->tsd/dot_general | solution.py:84
  631.6 24.8 %copy.127 = f32[256,4,48,128]{3,2,0,1:T(8,128)} copy(f32[256,4,48,128]{0,3,2,1:T(8,128)} %bitcast.184) | data formatting | bytes 50331648 | tf_op jit(solution)/shard_map/reshape | solution.py:57
  656.4 16.1 %convert_bitcast_fusion.1 = bf16[256,4,16,128]{3,2,0,1:T(8,128)(2,1)} fusion(f32[256,4,48,128]{3,2,0,1:T(8,128)} %copy.127, f32[4,48]{1,0:T(4,128)S(1)} %copy-done.9, s32[4,48]{1,0:T(4,128)S(1)} %copy-done.10), kind=kOutput, calls=%fused_computation.50 | convolution fusion | flops 1210062848 | bytes 29361664 | tf_op jit(solution)/shard_map/tgcn,gcr->tgrn/dot_general | solution.py:58
  672.6 7.5 copy.128
  680.1 15.2 %multiply_convert_fusion.1 = bf16[192,128,128]{2,1,0:T(8,128)(2,1)} fusion(f32[192]{0:T(256)S(1)} %convert_element_type.75, bf16[192,256,128]{2,1,0:T(8,128)(2,1)} %gather_fusion.8, pred[192]{0:T(512)(128)(4,1)S(1)} %copy-done.11, bf16[192,256,128]{2,1,0:T(8,128)(2,1)} %gather_fusion.3, pred[192]{0:T(512)(128)(4,1)S(1)} %copy-done.13), kind=kOutput, calls=%fused_computation.34 | convolution fusion | flops 1629487104 | bytes 31458432 | tf_op jit(solution)/shard_map/tsk,tsn->skn/dot_general | solution.py:114
  695.3 14.2 %multiply_convert_fusion.2 = bf16[192,128,128]{2,1,0:T(8,128)(2,1)} fusion(f32[192]{0:T(256)S(1)} %convert_element_type.75, bf16[192,256,128]{2,1,0:T(8,128)(2,1)} %gather_fusion.7, pred[192]{0:T(512)(128)(4,1)S(1)} %copy-done.11, bf16[192,256,128]{2,1,0:T(8,128)(2,1)} %gather_fusion.3, pred[192]{0:T(512)(128)(4,1)S(1)} %copy-done.13), kind=kOutput, calls=%fused_computation.35 | convolution fusion | flops 1629487104 | bytes 31458432 | tf_op jit(solution)/shard_map/tsk,tsn->skn/dot_general | solution.py:110
  709.6 13.3 %multiply_convert_fusion = bf16[192,128,128]{2,1,0:T(8,128)(2,1)} fusion(f32[192]{0:T(256)S(1)} %convert_element_type.75, bf16[192,256,128]{2,1,0:T(8,128)(2,1)} %gather_fusion.6, pred[192]{0:T(512)(128)(4,1)S(1)} %copy-done.13, bf16[192,256,128]{2,1,0:T(8,128)(2,1)} %gather_fusion.5, pred[192]{0:T(512)(128)(4,1)S(1)} %copy-done.11), kind=kOutput, calls=%fused_computation.33 | convolution fusion | flops 1629487104 | bytes 31458432 | tf_op jit(solution)/shard_map/tsf,tsd->sfd/dot_general | solution.py:96
  723.7 2.0 copy.142
  725.7 4.8 reduce-scatter.6.cloned.1.call-done
  730.5 2.0 copy.141
  732.5 111.6 %reduce-scatter.12.cloned.1.call-done = bf16[48,128,128]{2,1,0:T(8,128)(2,1)} async-done(((bf16[192,128,128]{2,1,0:T(8,128)(2,1)}), bf16[48,128,128]{2,1,0:T(8,128)(2,1)}) %reduce-scatter.12.cloned.1.call-update) | async-done | bytes 1572880 | tf_op jit(solution)/shard_map/reduce_scatter | solution.py:121
  844.2 4.9 broadcast.83.clone.1
  849.1 7.0 scatter_fusion.1
  856.1 12.5 %copy.157 = bf16[16,128,14,128]{3,2,1,0:T(8,128)(2,1)} copy(bf16[16,128,14,128]{3,1,2,0:T(8,128)(2,1)} %bitcast.186) | data formatting | bytes 14680064
  868.5 10.2 copy.178
  878.7 79.6 %reduce-scatter.10.cloned.1.call-done = bf16[48,128,128]{2,1,0:T(8,128)(2,1)} async-done(((bf16[192,128,128]{2,1,0:T(8,128)(2,1)}), bf16[48,128,128]{2,1,0:T(8,128)(2,1)}) %reduce-scatter.10.cloned.1.call-update) | async-done | bytes 1572880 | tf_op jit(solution)/shard_map/reduce_scatter | solution.py:118
  958.4 4.9 broadcast.83.clone
  963.3 7.2 scatter_fusion
  970.4 12.5 %copy.156 = bf16[16,128,14,128]{3,2,1,0:T(8,128)(2,1)} copy(bf16[16,128,14,128]{3,1,2,0:T(8,128)(2,1)} %bitcast.187) | data formatting | bytes 14680064
  982.9 10.2 copy.179
  993.1 78.7 %reduce-scatter.14.cloned.1.call-done = bf16[48,128,128]{2,1,0:T(8,128)(2,1)} async-done(((bf16[192,128,128]{2,1,0:T(8,128)(2,1)}), bf16[48,128,128]{2,1,0:T(8,128)(2,1)}) %reduce-scatter.14.cloned.1.call-update) | async-done | bytes 1572880 | tf_op jit(solution)/shard_map/reduce_scatter | solution.py:99
  1071.8 4.9 broadcast.83.clone.2
  1076.7 6.7 scatter_fusion.2
  1083.4 9.1 copy.140
  1092.5 6.8 copy.177
  (75 shorter events, 6.2 us)
Async XLA Ops:
  7.2 4.3 copy-start
  7.2 93.5 %all-gather.10.cloned.1.call-start = ((), (), s32[]{:S(2)}) async-start(), calls=%async_computation.7 | async-start | bytes 4718592 | tf_op jit(solution)/shard_map/all_gather | solution.py:68
  9.3 97.7 %all-gather.14.cloned.1.call-start = ((), (), s32[]{:S(2)}) async-start(), calls=%async_computation.10 | async-start | bytes 4718592 | tf_op jit(solution)/shard_map/all_gather | solution.py:90
  11.4 205.4 %all-gather.12.cloned.1.call-start = ((), (), s32[]{:S(2)}) async-start(), calls=%async_computation.8 | async-start | bytes 7864320 | tf_op jit(solution)/shard_map/all_gather | solution.py:72
  58.6 22.4 %copy-start.14 = (s32[4,48]{1,0:T(4,128)}, s32[4,48]{1,0:T(4,128)S(1)}, u32[]{:S(2)}) copy-start(s32[4,48]{1,0:T(4,128)S(1)} %get-tuple-element.42) | copy-start | bytes 2308
  58.6 41.4 %copy-start.8 = (f32[4,48]{1,0:T(4,128)}, f32[4,48]{1,0:T(4,128)S(1)}, u32[]{:S(2)}) copy-start(f32[4,48]{1,0:T(4,128)S(1)} %get-tuple-element.40) | copy-start | bytes 2308
  98.6 233.8 %all-gather.8.cloned.1.call-start = ((), (), s32[]{:S(2)}) async-start(), calls=%async_computation.6 | async-start | bytes 7864320 | tf_op jit(solution)/shard_map/all_gather | solution.py:71
  99.2 348.3 %all-gather.6.cloned.1.call-start = ((), (), s32[]{:S(2)}) async-start(), calls=%async_computation.5 | async-start | bytes 7864320 | tf_op jit(solution)/shard_map/all_gather | solution.py:81
  99.7 623.9 %reduce-scatter.8.cloned.1.call-start = ((), (), s32[]{:S(2)}) async-start(), calls=%async_computation.11 | async-start | bytes 4718592 | tf_op jit(solution)/shard_map/reduce_scatter | solution.py:131
  100.7 346.7 %copy-start.12 = (pred[192]{0:T(512)(128)(4,1)}, pred[192]{0:T(512)(128)(4,1)S(1)}, u32[]{:S(2)}) copy-start(pred[192]{0:T(512)(128)(4,1)S(1)} %get-tuple-element.47) | copy-start | bytes 580
  373.6 17.0 %copy-start.2 = (f32[256,192,128]{2,1,0:T(8,128)S(1)}, f32[256,192,128]{2,1,0:T(8,128)}, u32[]{:S(2)}) copy-start(f32[256,192,128]{2,1,0:T(8,128)} %copy.119) | copy-start | bytes 75497472
  486.1 15.2 %copy-start.3 = (f32[14,256,128]{2,0,1:T(8,128)S(1)}, f32[14,256,128]{2,0,1:T(8,128)}, u32[]{:S(2)}) copy-start(f32[14,256,128]{2,0,1:T(8,128)} %fusion.60) | copy-start | bytes 5505028
  486.1 15.2 %copy-start.4 = (f32[14,256,128]{2,0,1:T(8,128)S(1)}, f32[14,256,128]{2,0,1:T(8,128)}, u32[]{:S(2)}) copy-start(f32[14,256,128]{2,0,1:T(8,128)} %fusion.62) | copy-start | bytes 5505028
  511.6 8.0 copy-start.11
  557.8 24.8 %copy-start.9 = (f32[4,48]{1,0:T(4,128)S(1)}, f32[4,48]{1,0:T(4,128)}, u32[]{:S(2)}) copy-start(f32[4,48]{1,0:T(4,128)} %copy-done.8) | copy-start | bytes 2308
  557.8 24.8 %copy-start.10 = (s32[4,48]{1,0:T(4,128)S(1)}, s32[4,48]{1,0:T(4,128)}, u32[]{:S(2)}) copy-start(s32[4,48]{1,0:T(4,128)} %get-tuple-element.33) | copy-start | bytes 2308
  606.2 124.3 %reduce-scatter.6.cloned.1.call-start = ((), (), s32[]{:S(2)}) async-start(), calls=%async_computation.9 | async-start | bytes 4718592 | tf_op jit(solution)/shard_map/reduce_scatter | solution.py:86
  672.6 7.5 copy-start.13
  680.1 164.1 %reduce-scatter.12.cloned.1.call-start = ((), (), s32[]{:S(2)}) async-start(), calls=%async_computation.13 | async-start | bytes 7864320 | tf_op jit(solution)/shard_map/reduce_scatter | solution.py:121
  695.3 263.1 %reduce-scatter.10.cloned.1.call-start = ((), (), s32[]{:S(2)}) async-start(), calls=%async_computation.12 | async-start | bytes 7864320 | tf_op jit(solution)/shard_map/reduce_scatter | solution.py:118
  709.6 362.2 %reduce-scatter.14.cloned.1.call-start = ((), (), s32[]{:S(2)}) async-start(), calls=%async_computation.14 | async-start | bytes 7864320 | tf_op jit(solution)/shard_map/reduce_scatter | solution.py:99
  844.2 4.9 copy-start.5
  958.3 4.9 copy-start.6
  1071.8 4.9 copy-start.7
  1092.5 6.8 copy-start.1
Sparse Core Ops, SparseCore 0:
  10.5 39.4 all-gather.9
  52.4 36.7 all-gather.13
  98.7 118.0 all-gather.11
  218.8 113.5 all-gather.7
  333.8 113.5 all-gather.5
  606.3 49.7 reduce-scatter.7
  680.2 50.2 reduce-scatter.5
  733.4 110.7 reduce-scatter.11
  847.0 111.2 reduce-scatter.9
  960.5 111.2 reduce-scatter.13
where the time goes:
time: 1120 us; the launch traced here: 1110 us
  waiting for transfers between devices  476 us (42%)
  local copies, waits for them, and re-layouts  382 us (34%)
  matrix products  222 us (20%)
  between operations  14.6 us (1%)
    reduce_scatter x1, waiting for transfers between devices, on_device(): lax.psum_scatter(up_terms.astype(jnp.bfloat16), 'row', scatter_dimension=...  112 us
    all_gather x1, waiting for transfers between devices, on_device(): lax.all_gather(packed_up, 'row', axis=0, tiled=True)  82.2 us
    reduce_scatter x1, waiting for transfers between devices, on_device(): lax.psum_scatter(gate_terms.astype(jnp.bfloat16), 'row', scatter_dimensio...  79.6 us
    reduce_scatter x1, waiting for transfers between devices, on_device(): lax.psum_scatter(down_terms.astype(jnp.bfloat16), 'row', scatter_dimensio...  78.7 us
    all_gather x1, waiting for transfers between devices, on_device(): lax.all_gather(packed_gate, 'row', axis=0, tiled=True)  74.5 us
    unnamed x40, local copies, waits for them, and re-layouts  69.3 us
    reshape x2, local copies, waits for them, and re-layouts, sum_rows(): blocked = parts.reshape(tok_rows, row_count, capacity, BLK)  49.6 us
    dot_general x3, matrix products, sum_cols(): jnp.einsum('tsn,sj->tjn', parts, col_onehot, precision=highest)  45.4 us
  transfers between devices with their start and end apart: 10, of which 7 were waited for; matrix products, arithmetic and copies ran while one was open for 39% of the time, Pallas kernels for 0%

commit v1 on v0

v1 whole, which is shorter than its diff:
```python
import jax
import jax.numpy as jnp
from jax import lax
from jax.sharding import PartitionSpec as P

BLK = 128


def on_device(tokens, cotangent, gate_weight, up_weight, down_weight, tile_mask):
    row_count = lax.axis_size("row")
    col_count = lax.axis_size("col")
    row_index = lax.axis_index("row")
    col_index = lax.axis_index("col")
    tok_rows, tok_cols = tokens.shape
    block_rows, block_cols = gate_weight.shape
    row_tiles = block_rows // BLK
    col_tiles = block_cols // BLK
    piece = tok_rows // col_count
    all_rows = tok_rows * row_count
    f32, bf16 = jnp.float32, jnp.bfloat16

    block = lax.dynamic_slice(
        tile_mask, (row_index * row_tiles, col_index * col_tiles), (row_tiles, col_tiles)
    ).astype(bf16)
    spread_rows = (
        jnp.arange(block_rows)[:, None] // BLK == jnp.arange(row_tiles)[None, :]
    ).astype(bf16)
    spread_cols = (
        jnp.arange(col_tiles)[:, None] == jnp.arange(block_cols)[None, :] // BLK
    ).astype(bf16)
    wide = jnp.dot(block, spread_cols, preferred_element_type=f32).astype(bf16)
    full = jnp.dot(spread_rows, wide, preferred_element_type=f32).astype(bf16)
    wide_t = jnp.dot(spread_rows, block, preferred_element_type=f32).astype(bf16).T
    full_t = jnp.dot(spread_cols.T, wide_t, preferred_element_type=f32).astype(bf16)
    gate_w = jnp.where(full > 0, gate_weight, 0)
    up_w = jnp.where(full > 0, up_weight, 0)
    down_w = jnp.where(full_t > 0, down_weight, 0)

    def spread(x):
        x = lax.all_to_all(x, "col", split_axis=0, concat_axis=1, tiled=True)
        x = lax.all_to_all(x, "row", split_axis=1, concat_axis=0, tiled=True)
        return lax.all_gather(x, "col", axis=0, tiled=True)

    def collect(x):
        x = lax.psum_scatter(x, "col", scatter_dimension=0, tiled=True)
        x = lax.all_to_all(x, "row", split_axis=0, concat_axis=1, tiled=True)
        return lax.all_to_all(x, "col", split_axis=1, concat_axis=0, tiled=True)

    def nn(a, b):
        return lax.dot_general(a, b, (((1,), (0,)), ((), ())), preferred_element_type=f32)

    def nt(a, b):
        return lax.dot_general(a, b, (((1,), (1,)), ((), ())), preferred_element_type=f32)

    def tn(a, b):
        return lax.dot_general(a, b, (((0,), (0,)), ((), ())), preferred_element_type=f32)

    def row_sum(x):
        return lax.psum_scatter(x.astype(bf16), "row", scatter_dimension=0, tiled=True).astype(f32)

    def row_gather(x):
        return lax.all_gather(x, "row", axis=0, tiled=True)

    toks = spread(tokens)
    cots = spread(cotangent)
    gate = row_sum(nn(toks, gate_w))
    upper = row_sum(nn(toks, up_w))
    hidden_grad = row_sum(nt(cots, down_w))
    sig = jax.nn.sigmoid(gate)
    silu = gate * sig
    hidden = row_gather((silu * upper).astype(bf16))
    gate_cot = row_gather(
        (hidden_grad * upper * sig * (1.0 + gate * (1.0 - sig))).astype(bf16)
    )
    up_cot = row_gather((hidden_grad * silu).astype(bf16))
    output = collect(nn(hidden, down_w).astype(bf16))
    down_grad = jnp.where(full_t > 0, tn(hidden, cots), 0).astype(bf16)
    gate_grad = jnp.where(full > 0, tn(toks, gate_cot), 0).astype(bf16)
    input_grad = collect((nt(gate_cot, gate_w) + nt(up_cot, up_w)).astype(bf16))
    up_grad = jnp.where(full > 0, tn(toks, up_cot), 0).astype(bf16)
    return output, input_grad, gate_grad, up_grad, down_grad


def solution(mesh):
    return jax.shard_map(
        on_device,
        mesh=mesh,
        in_specs=(
            P("row", "col"),
            P("row", "col"),
            P("row", "col"),
            P("row", "col"),
            P("col", "row"),
            P(),
        ),
        out_specs=(
            P("row", "col"),
            P("row", "col"),
            P("row", "col"),
            P("row", "col"),
            P("col", "row"),
        ),
        check_vma=False,
    )
```

time: 1120 us -> 731 us (0.65)
  local copies, waits for them, and re-layouts: 382 us -> 6.78 us
  matrix products: 222 us -> 131 us
  blocking collectives: 0 us -> 65 us
  starting transfers between devices: 0.41 us -> 18.2 us
    transpose x8 -> x0, local copies, waits for them, and re-layouts: 110 us -> none  [the longest x1 24.8 us: on_device(): jnp.einsum('tsk,skn->tsn', token_tiles, gate_tiles, preferred_element_typ...]
    dot_general x14 -> x11, matrix products: 222 us -> 131 us  [the longest x3 42.1 us: nt(): lax.dot_general(a, b, (((1,), (1,)), ((), ())), preferred_element_type=f32)]
    reshape x8 -> x0, local copies, waits for them, and re-layouts: 90.3 us -> none  [the longest x2 49.6 us: sum_rows(): blocked = parts.reshape(tok_rows, row_count, capacity, BLK)]
    unnamed x40 -> x6, local copies, waits for them, and re-layouts: 69.3 us -> 1.6 us
    all_to_all x0 -> x4, blocking collectives: none -> 65 us  [the longest x2 34.4 us: spread(): x = lax.all_to_all(x, 'row', split_axis=1, concat_axis=0, tiled=True)]
    gather x11 -> x0, local copies, waits for them, and re-layouts: 61.3 us -> none  [the longest x1 10.5 us: on_device(): jnp.take(gathered_cot.reshape(tok_rows, all_row_tiles, BLK), tile_row, ax...]
    scatter x3 -> x0, local copies, waits for them, and re-layouts: 20.9 us -> none  [the longest x2 14.2 us: unpack_in(): dense = jnp.zeros((tile_count, BLK, BLK), jnp.bfloat16).at[own_order].set...]
    reduce_scatter x5, waiting for transfers between devices: 275 us -> 292 us  [the longest x3 201 us: row_sum(): lax.psum_scatter(x.astype(bf16), 'row', scatter_dimension=0, tiled=True)]
  transfers between devices with their start and end apart: 10 -> 14, of which waited for: 7 -> 9; matrix products, arithmetic and copies ran while one was open for 39% -> 19% of each run, Pallas kernels for 0% -> 0%
where the time goes in v1:
time: 731 us; the launch traced here: 724 us
  waiting for transfers between devices  485 us (66%)
  matrix products  131 us (18%)
  blocking collectives  65 us (9%)
  starting transfers between devices  18.2 us (2%)
  between operations  14.5 us (2%)
    reduce_scatter x3, waiting for transfers between devices, row_sum(): lax.psum_scatter(x.astype(bf16), 'row', scatter_dimension=0, tiled=True)  201 us
    all_gather x3, waiting for transfers between devices, row_gather(): return lax.all_gather(x, 'row', axis=0, tiled=True)  185 us
    reduce_scatter x2, waiting for transfers between devices, collect(): x = lax.psum_scatter(x, 'col', scatter_dimension=0, tiled=True)  91.2 us
    dot_general x3, matrix products, nt(): lax.dot_general(a, b, (((1,), (1,)), ((), ())), preferred_element_type=f32)  42.1 us
    dot_general x3, matrix products, tn(): lax.dot_general(a, b, (((0,), (0,)), ((), ())), preferred_element_type=f32)  40 us
    dot_general x3, matrix products, nn(): lax.dot_general(a, b, (((1,), (0,)), ((), ())), preferred_element_type=f32)  39.5 us
    all_to_all x2, blocking collectives, spread(): x = lax.all_to_all(x, 'row', split_axis=1, concat_axis=0, tiled=True)  34.4 us
    all_to_all x2, blocking collectives, spread(): x = lax.all_to_all(x, 'col', split_axis=0, concat_axis=1, tiled=True)  30.5 us
  transfers between devices with their start and end apart: 14, of which 9 were waited for; matrix products, arithmetic and copies ran while one was open for 19% of the time, Pallas kernels for 0%

profile of v1, /device:TPU:0, one launch (start us, length us, event | category | flops | bytes accessed | tf_op | source)
XLA Modules:
  0.0 724.4 jit_solution(4914351747478081704)
XLA Ops:
  7.2 0.0 all-gather.6.cloned.1.call-start
  7.2 15.1 %all_to_all.140 = bf16[8,32,1024]{2,1,0:T(8,128)(2,1)S(1)} all-to-all(bf16[8,32,1024]{2,1,0:T(8,128)(2,1)} %bitcast.54), channel_id=1, replica_groups=mesh['row'=4,'col'=8] {'col'}, dimensions={0} | all-to-all | bytes 1048576 | tf_op jit(solution)/shard_map/all_to_all | solution.py:40
  22.3 0.3 copy.31
  22.6 0.4 all_to_all.107
  23.0 0.3 copy.32
  23.3 0.0 copy-start.1
  23.3 18.6 %all_to_all.141 = bf16[32,4,2048]{2,0,1:T(8,128)(2,1)} all-to-all(bf16[32,4,2048]{2,0,1:T(8,128)(2,1)S(1)} %copy.32), channel_id=1, replica_groups=mesh['row'=4,'col'=8] {'row'}, dimensions={1} | all-to-all | bytes 1048576 | tf_op jit(solution)/shard_map/all_to_all | solution.py:41
  41.9 0.0 all-gather.6.cloned.1.call-update
  41.9 0.0 all-gather.10.cloned.1.call-start
  42.0 15.5 %all_to_all.142 = bf16[8,32,1024]{2,1,0:T(8,128)(2,1)S(1)} all-to-all(bf16[8,32,1024]{2,1,0:T(8,128)(2,1)S(1)} %bitcast.55), channel_id=1, replica_groups=mesh['row'=4,'col'=8] {'col'}, dimensions={0} | all-to-all | bytes 1048576 | tf_op jit(solution)/shard_map/all_to_all | solution.py:40
  57.5 0.3 copy.35
  57.8 0.4 all_to_all.121
  58.2 0.3 copy.36
  58.5 15.8 %all_to_all.143 = bf16[32,4,2048]{2,0,1:T(8,128)(2,1)} all-to-all(bf16[32,4,2048]{2,0,1:T(8,128)(2,1)S(1)} %copy.36), channel_id=1, replica_groups=mesh['row'=4,'col'=8] {'row'}, dimensions={1} | all-to-all | bytes 1048576 | tf_op jit(solution)/shard_map/all_to_all | solution.py:41
  74.3 0.0 all-gather.10.cloned.1.call-update
  74.3 0.0 reduce-scatter.6.cloned.1.call-start
  74.4 3.8 fusion.3
  78.2 13.2 %fusion.28 = bf16[1024,1792]{0,1:T(8,128)(2,1)} fusion(bf16[1024,2048]{1,0:T(8,128)(2,1)} %all-gather.6.cloned.1.call-done, pred[2048,1792]{1,0:T(32,128)(4,1)} %fusion.3, bf16[2048,1792]{1,0:T(8,128)(2,1)} %param.8), kind=kOutput, calls=%fused_computation.28 | convolution fusion | flops 7521697792 | bytes 18874368 | tf_op jit(solution)/shard_map/dot_general | solution.py:50
  91.5 0.0 reduce-scatter.6.cloned.1.call-update
  91.5 0.2 reduce-scatter.8.cloned.1.call-start
  91.7 13.1 %fusion.29 = bf16[1024,1792]{0,1:T(8,128)(2,1)} fusion(bf16[1024,2048]{1,0:T(8,128)(2,1)} %all-gather.6.cloned.1.call-done, pred[2048,1792]{1,0:T(32,128)(4,1)} %fusion.3, bf16[2048,1792]{1,0:T(8,128)(2,1)} %param.9), kind=kOutput, calls=%fused_computation.29 | convolution fusion | flops 7521697792 | bytes 18874368 | tf_op jit(solution)/shard_map/dot_general | solution.py:50
  104.8 0.0 reduce-scatter.8.cloned.1.call-update
  104.9 0.0 reduce-scatter.12.cloned.1.call-start
  104.9 5.3 fusion.2
  110.2 6.0 all-gather.10.cloned.1.call-done
  116.3 13.1 %fusion.25 = bf16[1024,1792]{0,1:T(8,128)(2,1)} fusion(bf16[1024,2048]{1,0:T(8,128)(2,1)} %all-gather.10.cloned.1.call-done, pred[1792,2048]{1,0:T(32,128)(4,1)} %fusion.2, bf16[1792,2048]{1,0:T(8,128)(2,1)} %param.10), kind=kOutput, calls=%fused_computation.27 | convolution fusion | flops 7521697792 | bytes 18874368 | tf_op jit(solution)/shard_map/dot_general | solution.py:53
  129.3 0.0 reduce-scatter.12.cloned.1.call-update
  129.3 0.0 all-gather.14.cloned.1.call-start
  129.4 57.6 %reduce-scatter.6.cloned.1.call-done = bf16[256,1792]{0,1:T(8,128)(2,1)} async-done(((bf16[1024,1792]{0,1:T(8,128)(2,1)}), bf16[256,1792]{0,1:T(8,128)(2,1)}) %reduce-scatter.6.cloned.1.call-update) | async-done | bytes 917520 | tf_op jit(solution)/shard_map/reduce_scatter | solution.py:59
  187.0 71.6 %reduce-scatter.8.cloned.1.call-done = bf16[256,1792]{0,1:T(8,128)(2,1)} async-done(((bf16[1024,1792]{0,1:T(8,128)(2,1)}), bf16[256,1792]{0,1:T(8,128)(2,1)}) %reduce-scatter.8.cloned.1.call-update) | async-done | bytes 917520 | tf_op jit(solution)/shard_map/reduce_scatter | solution.py:59
  258.6 71.5 %reduce-scatter.12.cloned.1.call-done = bf16[256,1792]{0,1:T(8,128)(2,1)} async-done(((bf16[1024,1792]{0,1:T(8,128)(2,1)}), bf16[256,1792]{0,1:T(8,128)(2,1)}) %reduce-scatter.12.cloned.1.call-update) | async-done | bytes 917520 | tf_op jit(solution)/shard_map/reduce_scatter | solution.py:59
  330.1 4.3 fusion.35
  334.5 0.0 all-gather.14.cloned.1.call-update
  334.5 0.0 all-gather.12.cloned.1.call-start
  334.5 0.7 all-gather.12.cloned.1.call-update
  335.2 0.0 all-gather.8.cloned.1.call-start
  335.3 0.7 all-gather.8.cloned.1.call-update
  336.0 0.3 reduce-scatter.14.cloned.1.call-start
  336.2 70.8 %all-gather.14.cloned.1.call-done = bf16[1024,1792]{0,1:T(8,128)(2,1)} async-done(((bf16[256,1792]{0,1:T(8,128)(2,1)}), bf16[1024,1792]{0,1:T(8,128)(2,1)}) %all-gather.14.cloned.1.call-update) | async-done | bytes 3670032 | tf_op jit(solution)/shard_map/all_gather | solution.py:62
  407.0 13.8 %fusion.8 = f32[1024,2048]{1,0:T(8,128)} fusion(bf16[1024,1792]{0,1:T(8,128)(2,1)} %all-gather.14.cloned.1.call-done, pred[2048,1792]{1,0:T(32,128)(4,1)} %fusion.3, bf16[2048,1792]{1,0:T(8,128)(2,1)} %param.9), kind=kOutput, calls=%fused_computation.14 | convolution fusion | flops 7519862784 | bytes 23068672 | tf_op jit(solution)/shard_map/dot_general | solution.py:53
  420.8 58.5 %all-gather.12.cloned.1.call-done = bf16[1024,1792]{0,1:T(8,128)(2,1)} async-done(((bf16[256,1792]{0,1:T(8,128)(2,1)}), bf16[1024,1792]{0,1:T(8,128)(2,1)}) %all-gather.12.cloned.1.call-update) | async-done | bytes 3670032 | tf_op jit(solution)/shard_map/all_gather | solution.py:62
  479.3 15.3 %add_convert_fusion = bf16[1024,2048]{1,0:T(8,128)(2,1)} fusion(f32[1024,2048]{1,0:T(8,128)} %fusion.8, bf16[1024,1792]{0,1:T(8,128)(2,1)} %all-gather.12.cloned.1.call-done, pred[2048,1792]{1,0:T(32,128)(4,1)} %fusion.3, bf16[2048,1792]{1,0:T(8,128)(2,1)} %param.8), kind=kOutput, calls=%fused_computation.5 | convolution fusion | flops 7524057088 | bytes 27262976 | tf_op jit(solution)/shard_map/dot_general | solution.py:53
  494.6 0.0 reduce-scatter.14.cloned.1.call-update
  494.7 0.4 reduce-scatter.10.cloned.1.call-start
  495.1 56.0 %all-gather.8.cloned.1.call-done = bf16[1024,1792]{0,1:T(8,128)(2,1)} async-done(((bf16[256,1792]{0,1:T(8,128)(2,1)}), bf16[1024,1792]{0,1:T(8,128)(2,1)}) %all-gather.8.cloned.1.call-update) | async-done | bytes 3670032 | tf_op jit(solution)/shard_map/all_gather | solution.py:62
  551.1 13.1 %fusion.18 = bf16[1024,2048]{1,0:T(8,128)(2,1)} fusion(bf16[1024,1792]{0,1:T(8,128)(2,1)} %all-gather.8.cloned.1.call-done, pred[1792,2048]{1,0:T(32,128)(4,1)} %fusion.2, bf16[1792,2048]{1,0:T(8,128)(2,1)} %param.10), kind=kOutput, calls=%fused_computation.20 | convolution fusion | flops 7521959936 | bytes 18874368 | tf_op jit(solution)/shard_map/dot_general | solution.py:50
  564.2 0.0 reduce-scatter.10.cloned.1.call-update
  564.3 40.3 %reduce-scatter.14.cloned.1.call-done = bf16[128,2048]{1,0:T(8,128)(2,1)} async-done(((bf16[1024,2048]{1,0:T(8,128)(2,1)}), bf16[128,2048]{1,0:T(8,128)(2,1)}) %reduce-scatter.14.cloned.1.call-update) | async-done | bytes 524304 | tf_op jit(solution)/shard_map/reduce_scatter | solution.py:45
  604.6 4.6 all-to-all-start.6
  609.2 50.9 %reduce-scatter.10.cloned.1.call-done = bf16[128,2048]{1,0:T(8,128)(2,1)} async-done(((bf16[1024,2048]{1,0:T(8,128)(2,1)}), bf16[128,2048]{1,0:T(8,128)(2,1)}) %reduce-scatter.10.cloned.1.call-update) | async-done | bytes 524304 | tf_op jit(solution)/shard_map/reduce_scatter | solution.py:45
  660.1 4.6 all-to-all-start.2
  664.7 13.1 %select_convert_fusion = bf16[1792,2048]{1,0:T(8,128)(2,1)} fusion(pred[1792,2048]{1,0:T(32,128)(4,1)} %fusion.2, bf16[1024,1792]{0,1:T(8,128)(2,1)} %all-gather.8.cloned.1.call-done, bf16[1024,2048]{1,0:T(8,128)(2,1)} %all-gather.10.cloned.1.call-done), kind=kOutput, calls=%fused_computation.4 | convolution fusion | flops 7523532800 | bytes 18874368 | tf_op jit(solution)/shard_map/dot_general | solution.py:56
  677.8 0.4 copy.37
  678.2 0.1 all_to_all.128
  678.3 1.1 copy.38
  679.4 3.7 all-to-all-start.7
  683.1 13.4 %fusion = bf16[2048,1792]{1,0:T(8,128)(2,1)} fusion(pred[2048,1792]{1,0:T(32,128)(4,1)} %fusion.3, bf16[1024,1792]{0,1:T(8,128)(2,1)} %all-gather.14.cloned.1.call-done, bf16[1024,2048]{1,0:T(8,128)(2,1)} %all-gather.6.cloned.1.call-done), kind=kOutput, calls=%fused_computation.1 | convolution fusion | flops 7523532800 | bytes 18874368 | tf_op jit(solution)/shard_map/dot_general | solution.py:56
  696.5 0.4 copy.33
  696.9 0.1 all_to_all.114
  697.1 1.1 copy.34
  698.1 4.2 all-to-all-start.3
  702.3 13.4 %fusion.1 = bf16[2048,1792]{1,0:T(8,128)(2,1)} fusion(pred[2048,1792]{1,0:T(32,128)(4,1)} %fusion.3, bf16[1024,1792]{0,1:T(8,128)(2,1)} %all-gather.12.cloned.1.call-done, bf16[1024,2048]{1,0:T(8,128)(2,1)} %all-gather.6.cloned.1.call-done), kind=kOutput, calls=%fused_computation.3 | convolution fusion | flops 7523532800 | bytes 18874368 | tf_op jit(solution)/shard_map/dot_general | solution.py:56
  715.7 0.8 copy.56
  716.5 0.8 copy.57
  (10 shorter events, 0.0 us)
Async XLA Ops:
  7.2 34.8 %copy-start = (bf16[256,1024]{1,0:T(8,128)(2,1)S(1)}, bf16[256,1024]{1,0:T(8,128)(2,1)}, u32[]{:S(2)}) copy-start(bf16[256,1024]{1,0:T(8,128)(2,1)} %param.7) | copy-start | bytes 1572868
  7.2 71.1 %all-gather.6.cloned.1.call-start = ((), (), s32[]{:S(2)}) async-start(), calls=%async_computation.13 | async-start | bytes 4718592 | tf_op jit(solution)/shard_map/all_gather | solution.py:42
  23.3 51.1 %copy-start.1 = (s32[64,112]{1,0:T(8,128)S(1)}, s32[64,112]{1,0:T(8,128)}, u32[]{:S(2)}) copy-start(s32[64,112]{1,0:T(8,128)} %param.11) | copy-start | bytes 86020
  41.9 74.3 %all-gather.10.cloned.1.call-start = ((), (), s32[]{:S(2)}) async-start(), calls=%async_computation.18 | async-start | bytes 4718592 | tf_op jit(solution)/shard_map/all_gather | solution.py:42
  74.3 112.7 %reduce-scatter.6.cloned.1.call-start = ((), (), s32[]{:S(2)}) async-start(), calls=%async_computation.14 | async-start | bytes 4587520 | tf_op jit(solution)/shard_map/reduce_scatter | solution.py:59
  91.5 167.1 %reduce-scatter.8.cloned.1.call-start = ((), (), s32[]{:S(2)}) async-start(), calls=%async_computation.15 | async-start | bytes 4587520 | tf_op jit(solution)/shard_map/reduce_scatter | solution.py:59
  104.9 225.2 %reduce-scatter.12.cloned.1.call-start = ((), (), s32[]{:S(2)}) async-start(), calls=%async_computation.19 | async-start | bytes 4587520 | tf_op jit(solution)/shard_map/reduce_scatter | solution.py:59
  129.3 277.7 %all-gather.14.cloned.1.call-start = ((), (), s32[]{:S(2)}) async-start(), calls=%async_computation.21 | async-start | bytes 4587520 | tf_op jit(solution)/shard_map/all_gather | solution.py:62
  334.5 144.9 %all-gather.12.cloned.1.call-start = ((), (), s32[]{:S(2)}) async-start(), calls=%async_computation.20 | async-start | bytes 4587520 | tf_op jit(solution)/shard_map/all_gather | solution.py:62
  335.2 215.9 %all-gather.8.cloned.1.call-start = ((), (), s32[]{:S(2)}) async-start(), calls=%async_computation.16 | async-start | bytes 4587520 | tf_op jit(solution)/shard_map/all_gather | solution.py:62
  336.0 268.6 %reduce-scatter.14.cloned.1.call-start = ((), (), s32[]{:S(2)}) async-start(), calls=%async_computation.22 | async-start | bytes 4718592 | tf_op jit(solution)/shard_map/reduce_scatter | solution.py:45
  494.7 165.4 %reduce-scatter.10.cloned.1.call-start = ((), (), s32[]{:S(2)}) async-start(), calls=%async_computation.17 | async-start | bytes 4718592 | tf_op jit(solution)/shard_map/reduce_scatter | solution.py:45
  604.6 55.5 %all-to-all-start.6 = ((bf16[4,32,2048]{2,1,0:T(8,128)(2,1)}), bf16[4,32,2048]{2,1,0:T(8,128)(2,1)S(1)}, u32[]{:S(2)}, u32[]{:S(2)}) async-start(bf16[4,32,2048]{2,1,0:T(8,128)(2,1)} %bitcast.57), calls=%async_computation.11 | async-start | bytes 1048576 | tf_op jit(solution)/shard_map/all_to_all | solution.py:46
  660.1 19.3 %all-to-all-start.2 = ((bf16[4,32,2048]{2,1,0:T(8,128)(2,1)}), bf16[4,32,2048]{2,1,0:T(8,128)(2,1)S(1)}, u32[]{:S(2)}, u32[]{:S(2)}) async-start(bf16[4,32,2048]{2,1,0:T(8,128)(2,1)} %bitcast.56), calls=%async_computation.5 | async-start | bytes 1048576 | tf_op jit(solution)/shard_map/all_to_all | solution.py:46
  679.4 18.7 %all-to-all-start.7 = ((bf16[32,8,1024]{2,0,1:T(8,128)(2,1)}), bf16[32,8,1024]{2,0,1:T(8,128)(2,1)S(1)}, u32[]{:S(2)}, u32[]{:S(2)}) async-start(bf16[32,8,1024]{2,0,1:T(8,128)(2,1)} %copy.38), calls=%async_computation.12 | async-start | bytes 1048576 | tf_op jit(solution)/shard_map/all_to_all | solution.py:47
  698.1 17.6 %all-to-all-start.3 = ((bf16[32,8,1024]{2,0,1:T(8,128)(2,1)}), bf16[32,8,1024]{2,0,1:T(8,128)(2,1)S(1)}, u32[]{:S(2)}, u32[]{:S(2)}) async-start(bf16[32,8,1024]{2,0,1:T(8,128)(2,1)} %copy.34), calls=%async_computation.6 | async-start | bytes 1048576 | tf_op jit(solution)/shard_map/all_to_all | solution.py:47
Sparse Core Ops, SparseCore 0:
  42.0 35.5 all-gather.5
  79.5 36.7 all-gather.9
  118.6 68.3 reduce-scatter.5
  189.7 68.7 reduce-scatter.7
  261.3 68.7 reduce-scatter.11
  334.6 72.3 all-gather.13
  409.1 70.1 all-gather.11
  480.9 70.1 all-gather.7
  555.1 49.4 reduce-scatter.13
  608.7 51.3 reduce-scatter.9

commit v2 on v1

--- a/solution.py
+++ b/solution.py
@@ -1,9 +1,161 @@
+import functools
+
 import jax
 import jax.numpy as jnp
 from jax import lax
+from jax.experimental import pallas as pl
+from jax.experimental.pallas import tpu as pltpu
 from jax.sharding import PartitionSpec as P
 
 BLK = 128
+CHUNK = 16
+SKEW = 2
+MESH = pl.DeviceIdType.MESH
+
+
+def exchange_kernel(
+    count, chunks, gate_ref, up_ref, hg_ref, out_ref, part, rs_send, rs_recv, bc_send, bc_recv
+):
+    me = lax.axis_index("row")
+    last = count - 1
+    ways = ((me, me - 1, me + 1), (last - me, me + 1, me - 1))
+    own = (gate_ref, up_ref, hg_ref)
+    f32, bf16 = jnp.float32, jnp.bfloat16
+
+    def sum_copy(place, device):
+        return pltpu.make_async_remote_copy(
+            src_ref=part.at[place],
+            dst_ref=part.at[place],
+            send_sem=rs_send.at[place],
+            recv_sem=rs_recv.at[place],
+            device_id={"row": device},
+            device_id_type=MESH,
+        )
+
+    def result_copy(place, device):
+        return pltpu.make_async_remote_copy(
+            src_ref=out_ref.at[:, place],
+            dst_ref=out_ref.at[:, place],
+            send_sem=bc_send.at[place],
+            recv_sem=bc_recv.at[place],
+            device_id={"row": device},
+            device_id_type=MESH,
+        )
+
+    barrier = pltpu.get_barrier_semaphore()
+    for ok, device in ((me > 0, me - 1), (me < last, me + 1)):
+
+        @pl.when(ok)
+        def _():
+            pl.semaphore_signal(barrier, inc=1, device_id={"row": device}, device_id_type=MESH)
+
+    ends = jnp.logical_or(me == 0, me == last)
+
+    @pl.when(ends)
+    def _():
+        pl.semaphore_wait(barrier, 1)
+
+    @pl.when(jnp.logical_not(ends))
+    def _():
+        pl.semaphore_wait(barrier, 2)
+
+    def sums_of(way, step):
+        pos, toward, away = ways[way]
+        chunk = step - SKEW * (last - pos)
+        place = way * chunks + jnp.clip(chunk, 0, chunks - 1)
+        active = jnp.logical_and(chunk >= 0, chunk < chunks)
+
+        @pl.when(jnp.logical_and(active, pos == last))
+        def _():
+            for k in range(3):
+                part[place, k] = own[k][place]
+            sum_copy(place, toward).start()
+
+        @pl.when(jnp.logical_and(active, jnp.logical_and(pos > 0, pos < last)))
+        def _():
+            sum_copy(place, away).wait_recv()
+            for k in range(3):
+                part[place, k] = (part[place, k].astype(f32) + own[k][place].astype(f32)).astype(
+                    bf16
+                )
+            sum_copy(place, toward).start()
+
+        @pl.when(jnp.logical_and(active, pos == 0))
+        def _():
+            sum_copy(place, away).wait_recv()
+            gate, upper, hidden_grad = (
+                part[place, k].astype(f32) + own[k][place].astype(f32) for k in range(3)
+            )
+            sig = jax.nn.sigmoid(gate)
+            silu = gate * sig
+            out_ref[0, place] = (silu * upper).astype(bf16)
+            out_ref[1, place] = (
+                hidden_grad * upper * sig * (1.0 + gate * (1.0 - sig))
+            ).astype(bf16)
+            out_ref[2, place] = (hidden_grad * silu).astype(bf16)
+            result_copy(place, away).start()
+
+    def results_of(way, step):
+        pos, toward, away = ways[way]
+        chunk = step - SKEW * (last + pos)
+        place = way * chunks + jnp.clip(chunk, 0, chunks - 1)
+        active = jnp.logical_and(chunk >= 0, chunk < chunks)
+
+        @pl.when(jnp.logical_and(active, pos > 0))
+        def _():
+            result_copy(place, toward).wait_recv()
+
+        @pl.when(jnp.logical_and(active, jnp.logical_and(pos > 0, pos < last)))
+        def _():
+            result_copy(place, away).start()
+
+    def one_step(step, carry):
+        for way in range(2):
+            results_of(way, step)
+            sums_of(way, step)
+        return carry
+
+    lax.fori_loop(0, chunks + 2 * SKEW * last, one_step, 0)
+
+    def sent(chunk, carry):
+        for way in range(2):
+            pos, toward, away = ways[way]
+            place = way * chunks + chunk
+
+            @pl.when(pos > 0)
+            def _():
+                sum_copy(place, toward).wait_send()
+
+            @pl.when(pos < last)
+            def _():
+                result_copy(place, away).wait_send()
+
+        return carry
+
+    lax.fori_loop(0, chunks, sent, 0)
+
+
+def exchange(gate, upper, hidden_grad):
+    count = lax.axis_size("row")
+    rows, cols = gate.shape
+    places = rows // CHUNK
+    chunks = places // 2
+    shape = (places, CHUNK, cols)
+    out = pl.pallas_call(
+        functools.partial(exchange_kernel, count, chunks),
+        out_shape=jax.ShapeDtypeStruct((3,) + shape, jnp.bfloat16),
+        in_specs=[pl.BlockSpec(memory_space=pltpu.VMEM)] * 3,
+        out_specs=pl.BlockSpec(memory_space=pltpu.VMEM),
+        scratch_shapes=[pltpu.VMEM((places, 3, CHUNK, cols), jnp.bfloat16)]
+        + [pltpu.SemaphoreType.DMA((places,))] * 4,
+        compiler_params=pltpu.CompilerParams(
+            collective_id=0, has_side_effects=True, vmem_limit_bytes=48 * 1024 * 1024
+        ),
+        cost_estimate=pl.CostEstimate(
+            flops=40 * rows * cols, bytes_accessed=12 * rows * cols, transcendentals=rows * cols
+        ),
+    )(gate.reshape(shape), upper.reshape(shape), hidden_grad.reshape(shape))
+    return tuple(out[k].reshape(rows, cols) for k in range(3))
 
 
 def on_device(tokens, cotangent, gate_weight, up_weight, down_weight, tile_mask):
@@ -36,10 +188,11 @@
     up_w = jnp.where(full > 0, up_weight, 0)
     down_w = jnp.where(full_t > 0, down_weight, 0)
 
-    def spread(x):
-        x = lax.all_to_all(x, "col", split_axis=0, concat_axis=1, tiled=True)
-        x = lax.all_to_all(x, "row", split_axis=1, concat_axis=0, tiled=True)
-        return lax.all_gather(x, "col", axis=0, tiled=True)
+    both = jnp.stack([tokens, cotangent])
+    both = lax.all_to_all(both, "col", split_axis=1, concat_axis=2, tiled=True)
+    both = lax.all_to_all(both, "row", split_axis=2, concat_axis=1, tiled=True)
+    toks = lax.all_gather(both[0], "col", axis=0, tiled=True)
+    cots = lax.all_gather(both[1], "col", axis=0, tiled=True)
 
     def collect(x):
         x = lax.psum_scatter(x, "col", scatter_dimension=0, tiled=True)
@@ -55,24 +208,9 @@
     def tn(a, b):
         return lax.dot_general(a, b, (((0,), (0,)), ((), ())), preferred_element_type=f32)
 
-    def row_sum(x):
-        return lax.psum_scatter(x.astype(bf16), "row", scatter_dimension=0, tiled=True).astype(f32)
-
-    def row_gather(x):
-        return lax.all_gather(x, "row", axis=0, tiled=True)
-
-    toks = spread(tokens)
-    cots = spread(cotangent)
-    gate = row_sum(nn(toks, gate_w))
-    upper = row_sum(nn(toks, up_w))
-    hidden_grad = row_sum(nt(cots, down_w))
-    sig = jax.nn.sigmoid(gate)
-    silu = gate * sig
-    hidden = row_gather((silu * upper).astype(bf16))
-    gate_cot = row_gather(
-        (hidden_grad * upper * sig * (1.0 + gate * (1.0 - sig))).astype(bf16)
+    hidden, gate_cot, up_cot = exchange(
+        nn(toks, gate_w).astype(bf16), nn(toks, up_w).astype(bf16), nt(cots, down_w).astype(bf16)
     )
-    up_cot = row_gather((hidden_grad * silu).astype(bf16))
     output = collect(nn(hidden, down_w).astype(bf16))
     down_grad = jnp.where(full_t > 0, tn(hidden, cots), 0).astype(bf16)
     gate_grad = jnp.where(full > 0, tn(toks, gate_cot), 0).astype(bf16)

time: 731 us -> 639 us (0.87)
  waiting for transfers between devices: 485 us -> 114 us
  Pallas kernels: 0 us -> 269 us
  local copies, waits for them, and re-layouts: 6.78 us -> 43.3 us
  blocking collectives: 65 us -> 50.1 us
    pallas_call x0 -> x1, Pallas kernels: none -> 269 us  [exchange(): pl.pallas_call(functools.partial(exchange_kernel, count, chunks), out_sha...]
    reduce_scatter x3 -> x0, waiting for transfers between devices: 201 us -> none  [row_sum(): lax.psum_scatter(x.astype(bf16), 'row', scatter_dimension=0, tiled=True)]
    all_gather x5 -> x2, waiting for transfers between devices: 191 us -> 36.9 us  [the longest x1 24.3 us: on_device(): toks = lax.all_gather(both[0], 'col', axis=0, tiled=True)]
    all_to_all x4 -> x2, blocking collectives: 65 us -> 50.1 us  [the longest x1 29.8 us: on_device(): both = lax.all_to_all(both, 'row', split_axis=2, concat_axis=1, tiled=True)]
    reduce_scatter x2, waiting for transfers between devices: 91.2 us -> 77.5 us  [collect(): x = lax.psum_scatter(x, 'col', scatter_dimension=0, tiled=True)]
    all_to_all x6 -> x3, local copies, waits for them, and re-layouts: 1.96 us -> 15.2 us  [the longest x1 9.82 us: on_device(): both = lax.all_to_all(both, 'row', split_axis=2, concat_axis=1, tiled=True)]
    unnamed x6 -> x24, local copies, waits for them, and re-layouts: 1.6 us -> 14 us
    slice x0 -> x4, local copies, waits for them, and re-layouts: none -> 9.77 us  [the longest x1 7.11 us: exchange(): return tuple((out[k].reshape(rows, cols) for k in range(3)))]
  transfers between devices with their start and end apart: 14 -> 8, of which waited for: 9 -> 4; matrix products, arithmetic and copies ran while one was open for 19% -> 16% of each run, Pallas kernels for 0% -> 0%
where the time goes in v2:
time: 639 us; the launch traced here: 634 us
  Pallas kernels  269 us (42%)
  matrix products  124 us (19%)
  waiting for transfers between devices  114 us (18%)
  blocking collectives  50.1 us (8%)
  local copies, waits for them, and re-layouts  43.3 us (7%)
  starting transfers between devices  17.3 us (3%)
  between operations  14.1 us (2%)
    pallas_call x1, Pallas kernels, exchange(): pl.pallas_call(functools.partial(exchange_kernel, count, chunks), out_sha...  269 us
    reduce_scatter x2, waiting for transfers between devices, collect(): x = lax.psum_scatter(x, 'col', scatter_dimension=0, tiled=True)  77.5 us
    dot_general x3, matrix products, tn(): lax.dot_general(a, b, (((0,), (0,)), ((), ())), preferred_element_type=f32)  40.3 us
    dot_general x3, matrix products, nt(): lax.dot_general(a, b, (((1,), (1,)), ((), ())), preferred_element_type=f32)  38.4 us
    dot_general x3, matrix products, nn(): lax.dot_general(a, b, (((1,), (0,)), ((), ())), preferred_element_type=f32)  35.9 us
    all_to_all x1, blocking collectives, on_device(): both = lax.all_to_all(both, 'row', split_axis=2, concat_axis=1, tiled=True)  29.8 us
    all_gather x1, waiting for transfers between devices, on_device(): toks = lax.all_gather(both[0], 'col', axis=0, tiled=True)  24.3 us
    all_to_all x1, blocking collectives, on_device(): both = lax.all_to_all(both, 'col', split_axis=1, concat_axis=2, tiled=True)  20.3 us
  transfers between devices with their start and end apart: 8, of which 4 were waited for; matrix products, arithmetic and copies ran while one was open for 16% of the time, Pallas kernels for 0%

profile of v2, /device:TPU:0, one launch (start us, length us, event | category | flops | bytes accessed | tf_op | source)
XLA Modules:
  0.0 633.5 jit_solution(1582529853482922542)
XLA Ops:
  7.2 0.0 all-gather.3.cloned.1.call-start
  7.2 1.3 pad_maximum_fusion
  8.5 1.1 copy.27
  9.6 20.3 %all_to_all.103 = bf16[2,256,1024]{2,0,1:T(2,128)(2,1)S(1)} all-to-all(bf16[2,256,1024]{2,0,1:T(2,128)(2,1)S(1)} %copy.27), channel_id=1, replica_groups=mesh['row'=4,'col'=8] {'col'}, dimensions={1} | all-to-all | bytes 2097152 | tf_op jit(solution)/shard_map/all_to_all | solution.py:192
  29.9 0.6 copy.40
  30.5 4.8 copy.37
  35.3 5.6 reshape.114
  40.9 29.8 %all_to_all.104 = bf16[4,2,65536]{2,1,0:T(2,128)(2,1)S(1)} all-to-all(bf16[4,2,65536]{2,1,0:T(2,128)(2,1)S(1)} %reshape.114), channel_id=1, replica_groups=mesh['row'=4,'col'=8] {'row'}, dimensions={0} | all-to-all | bytes 2097152 | tf_op jit(solution)/shard_map/all_to_all | solution.py:193
  70.7 3.5 reshape.115
  74.2 9.8 %copy.38 = bf16[2,32,4,2048]{3,2,1,0:T(4,128)(2,1)S(1)} copy(bf16[2,32,4,2048]{1,0,3,2:T(2,128)(2,1)} %bitcast.43) | data formatting | bytes 2097152 | tf_op jit(solution)/shard_map/all_to_all | solution.py:193
  84.0 0.5 fusion.22
  84.5 1.1 copy.31
  85.6 0.0 all-gather.3.cloned.1.call-update
  85.6 0.0 all-gather.5.cloned.1.call-start
  85.6 1.1 copy.32
  86.7 0.0 all-gather.5.cloned.1.call-update
  86.7 0.2 reduce-scatter.3.cloned.1.call-start
  87.0 0.0 copy-done.4
  87.0 5.3 fusion
  92.3 3.9 fusion.1
  96.2 24.3 %all-gather.3.cloned.1.call-done = bf16[1024,2048]{1,0:T(8,128)(2,1)} async-done(((bf16[128,2048]{1,0:T(8,128)(2,1)}), bf16[1024,2048]{1,0:T(8,128)(2,1)}) %all-gather.3.cloned.1.call-update) | async-done | bytes 4194320 | tf_op jit(solution)/shard_map/all_gather | solution.py:194
  120.4 14.2 %convolution_convert_fusion.5 = bf16[1024,1792]{1,0:T(8,128)(2,1)} fusion(bf16[1024,2048]{1,0:T(8,128)(2,1)} %all-gather.3.cloned.1.call-done, pred[2048,1792]{1,0:T(32,128)(4,1)} %fusion.1, bf16[2048,1792]{1,0:T(8,128)(2,1)} %param.8), kind=kOutput, calls=%fused_computation.11 | convolution fusion | flops 7521697792 | bytes 18874368 | tf_op jit(solution)/shard_map/dot_general | solution.py:203
  134.6 0.0 copy-done.3
  134.6 0.0 copy-done.6
  134.6 12.3 %convolution_convert_fusion.4 = bf16[1024,1792]{1,0:T(8,128)(2,1)} fusion(bf16[1024,2048]{1,0:T(8,128)(2,1)S(1)} %copy-done.3, pred[2048,1792]{1,0:T(32,128)(4,1)S(1)} %copy-done.6, bf16[2048,1792]{1,0:T(8,128)(2,1)} %param.9), kind=kOutput, calls=%fused_computation.10 | convolution fusion | flops 7521697792 | bytes 18874368 | tf_op jit(solution)/shard_map/dot_general | solution.py:203
  147.0 12.7 %all-gather.5.cloned.1.call-done = bf16[1024,2048]{1,0:T(8,128)(2,1)} async-done(((bf16[128,2048]{1,0:T(8,128)(2,1)}), bf16[1024,2048]{1,0:T(8,128)(2,1)}) %all-gather.5.cloned.1.call-update) | async-done | bytes 4194320 | tf_op jit(solution)/shard_map/all_gather | solution.py:195
  159.6 14.5 %convolution_convert_fusion.3 = bf16[1024,1792]{1,0:T(8,128)(2,1)} fusion(bf16[1024,2048]{1,0:T(8,128)(2,1)} %all-gather.5.cloned.1.call-done, pred[1792,2048]{1,0:T(32,128)(4,1)} %fusion, bf16[1792,2048]{1,0:T(8,128)(2,1)} %param.10), kind=kOutput, calls=%fused_computation.9 | convolution fusion | flops 7521697792 | bytes 18874368 | tf_op jit(solution)/shard_map/dot_general | solution.py:206
  174.1 0.0 copy-done
  174.1 269.1 %shard_map.101 = bf16[3,64,16,1792]{3,2,1,0:T(8,128)(2,1)} custom-call(bf16[64,16,1792]{2,1,0:T(8,128)(2,1)S(1)} %bitcast.41, bf16[64,16,1792]{2,1,0:T(8,128)(2,1)} %bitcast.53, bf16[64,16,1792]{2,1,0:T(8,128)(2,1)} %bitcast.54), custom_call_target="tpu_custom_call" | custom-call | flops 73400320 | bytes 22020096 | tf_op jit(solution)/shard_map/pallas_call | solution.py:144
  443.2 0.0 slice-start.1
  443.2 0.0 copy-start.5
  443.2 7.1 %fusion.21 = (bf16[1,64,16,1792]{3,2,1,0:T(8,128)(2,1)}, bf16[1,64,16,1792]{3,2,1,0:T(8,128)(2,1)}, bf16[1,64,16,1792]{3,2,1,0:T(8,128)(2,1)S(1)}) fusion(bf16[3,64,16,1792]{3,2,1,0:T(8,128)(2,1)} %shard_map.101), kind=kLoop, calls=%fused_computation.47 | loop fusion | bytes 22020096 | tf_op jit(solution)/shard_map/slice | solution.py:158
  450.4 1.9 copy-done.2
  452.2 0.0 slice-done
  452.2 0.0 slice-done.1
  452.2 1.5 copy-done.5
  453.7 9.4 %convolution_convert_fusion.2 = bf16[1024,2048]{1,0:T(8,128)(2,1)} fusion(bf16[1024,1792]{1,0:T(8,128)(2,1)S(1)} %bitcast.51, pred[1792,2048]{1,0:T(32,128)(4,1)S(1)} %copy-done.5, bf16[1792,2048]{1,0:T(8,128)(2,1)S(1)} %bitcast.66), kind=kOutput, calls=%fused_computation.8 | convolution fusion | flops 7521959936 | bytes 18874368 | tf_op jit(solution)/shard_map/dot_general | solution.py:203
  463.1 0.0 reduce-scatter.3.cloned.1.call-update
  463.1 0.0 reduce-scatter.5.cloned.1.call-start
  463.2 0.0 copy-start.1
  463.2 12.3 %fusion.2 = f32[1024,2048]{1,0:T(8,128)S(1)} fusion(bf16[1024,1792]{1,0:T(8,128)(2,1)} %bitcast.49, pred[2048,1792]{1,0:T(32,128)(4,1)} %fusion.1, bf16[2048,1792]{1,0:T(8,128)(2,1)} %param.8), kind=kOutput, calls=%fused_computation.15 | convolution fusion | flops 7519862784 | bytes 23068672 | tf_op jit(solution)/shard_map/dot_general | solution.py:206
  475.6 11.6 %add_convert_fusion = bf16[1024,2048]{1,0:T(8,128)(2,1)} fusion(f32[1024,2048]{1,0:T(8,128)S(1)} %fusion.2, bf16[1024,1792]{1,0:T(8,128)(2,1)S(1)} %bitcast.48, pred[2048,1792]{1,0:T(32,128)(4,1)S(1)} %copy-done.7, bf16[2048,1792]{1,0:T(8,128)(2,1)} %param.9), kind=kOutput, calls=%fused_computation.3 | convolution fusion | flops 7524057088 | bytes 27262976 | tf_op jit(solution)/shard_map/dot_general | solution.py:206
  487.2 0.0 reduce-scatter.5.cloned.1.call-update
  487.2 26.5 %reduce-scatter.3.cloned.1.call-done = bf16[128,2048]{1,0:T(8,128)(2,1)} async-done(((bf16[1024,2048]{1,0:T(8,128)(2,1)}), bf16[128,2048]{1,0:T(8,128)(2,1)}) %reduce-scatter.3.cloned.1.call-update) | async-done | bytes 524304 | tf_op jit(solution)/shard_map/reduce_scatter | solution.py:198
  513.7 4.6 all-to-all-start.2
  518.3 50.9 %reduce-scatter.5.cloned.1.call-done = bf16[128,2048]{1,0:T(8,128)(2,1)} async-done(((bf16[1024,2048]{1,0:T(8,128)(2,1)}), bf16[128,2048]{1,0:T(8,128)(2,1)}) %reduce-scatter.5.cloned.1.call-update) | async-done | bytes 524304 | tf_op jit(solution)/shard_map/reduce_scatter | solution.py:198
  569.3 0.0 all-to-all-done.2
  569.3 4.6 all-to-all-start.4
  573.9 13.6 %select_convert_fusion = bf16[1792,2048]{1,0:T(8,128)(2,1)} fusion(pred[1792,2048]{1,0:T(32,128)(4,1)} %fusion, bf16[1024,1792]{1,0:T(8,128)(2,1)} %bitcast.52, bf16[1024,2048]{1,0:T(8,128)(2,1)} %all-gather.5.cloned.1.call-done), kind=kOutput, calls=%fused_computation | convolution fusion | flops 7523532800 | bytes 18874368 | tf_op jit(solution)/shard_map/dot_general | solution.py:209
  587.4 0.4 copy.33
  587.8 0.1 all_to_all.86
  588.0 1.1 copy.34
  589.0 0.0 all-to-all-done.4
  589.1 3.7 all-to-all-start.3
  592.7 13.4 %select_convert_fusion.2 = bf16[2048,1792]{1,0:T(8,128)(2,1)} fusion(pred[2048,1792]{1,0:T(32,128)(4,1)} %fusion.1, bf16[1024,2048]{1,0:T(8,128)(2,1)} %all-gather.3.cloned.1.call-done, bf16[1024,1792]{1,0:T(8,128)(2,1)} %bitcast.50), kind=kOutput, calls=%fused_computation.2 | convolution fusion | flops 7523532800 | bytes 18874368 | tf_op jit(solution)/shard_map/dot_general | solution.py:209
  606.1 0.4 copy.35
  606.5 0.1 all_to_all.93
  606.6 1.1 copy.36
  607.7 0.0 all-to-all-done.3
  607.7 4.1 all-to-all-start.5
  611.9 13.4 %select_convert_fusion.1 = bf16[2048,1792]{1,0:T(8,128)(2,1)} fusion(pred[2048,1792]{1,0:T(32,128)(4,1)} %fusion.1, bf16[1024,2048]{1,0:T(8,128)(2,1)} %all-gather.3.cloned.1.call-done, bf16[1024,1792]{1,0:T(8,128)(2,1)} %bitcast.47), kind=kOutput, calls=%fused_computation.1 | convolution fusion | flops 7523532800 | bytes 18874368 | tf_op jit(solution)/shard_map/dot_general | solution.py:209
  625.2 0.0 all-to-all-done.5
  625.2 0.8 copy.54
  626.0 0.8 copy.55
  (12 shorter events, 0.0 us)
Async XLA Ops:
  7.2 113.3 %all-gather.3.cloned.1.call-start = ((), (), s32[]{:S(2)}) async-start(), calls=%async_computation.8 | async-start | bytes 4718592 | tf_op jit(solution)/shard_map/all_gather | solution.py:194
  74.2 12.8 %copy-start.4 = (s32[64,112]{1,0:T(8,128)S(1)}, s32[64,112]{1,0:T(8,128)}, u32[]{:S(2)}) copy-start(s32[64,112]{1,0:T(8,128)} %param.11) | copy-start | bytes 86020
  85.6 74.1 %all-gather.5.cloned.1.call-start = ((), (), s32[]{:S(2)}) async-start(), calls=%async_computation.9 | async-start | bytes 4718592 | tf_op jit(solution)/shard_map/all_gather | solution.py:195
  86.7 427.0 %reduce-scatter.3.cloned.1.call-start = ((), (), s32[]{:S(2)}) async-start(), calls=%async_computation.10 | async-start | bytes 4718592 | tf_op jit(solution)/shard_map/reduce_scatter | solution.py:198
  120.4 14.2 %copy-start.3 = (bf16[1024,2048]{1,0:T(8,128)(2,1)S(1)}, bf16[1024,2048]{1,0:T(8,128)(2,1)}, u32[]{:S(2)}) copy-start(bf16[1024,2048]{1,0:T(8,128)(2,1)} %all-gather.3.cloned.1.call-done) | copy-start | bytes 12582916
  120.4 14.2 %copy-start.6 = (pred[2048,1792]{1,0:T(32,128)(4,1)S(1)}, pred[2048,1792]{1,0:T(32,128)(4,1)}, u32[]{:S(2)}) copy-start(pred[2048,1792]{1,0:T(32,128)(4,1)} %fusion.1) | copy-start | bytes 11010052
  159.6 14.5 %copy-start = (bf16[1024,1792]{1,0:T(8,128)(2,1)S(1)}, bf16[1024,1792]{1,0:T(8,128)(2,1)}, u32[]{:S(2)}) copy-start(bf16[1024,1792]{1,0:T(8,128)(2,1)} %convolution_convert_fusion.5) | copy-start | bytes 11010052
  174.1 278.1 %slice-start = ((s8[7340032]{0:T(1024)(128)(4,1)}), s8[3145728]{0:T(1024)(128)(4,1)S(1)}, s32[]{:S(2)}) async-start(s8[7340032]{0:T(1024)(128)(4,1)} %bitcast.65), calls=%async_computation.12 | async-start | bytes 6291456
  443.2 9.0 %slice-start.1 = ((s8[7340032]{0:T(1024)(128)(4,1)}), s8[4194304]{0:T(1024)(128)(4,1)S(1)}, s32[]{:S(2)}) async-start(s8[7340032]{0:T(1024)(128)(4,1)} %bitcast.65), calls=%async_computation.13 | async-start | bytes 8388608
  443.2 10.5 %copy-start.5 = (pred[1792,2048]{1,0:T(32,128)(4,1)S(1)}, pred[1792,2048]{1,0:T(32,128)(4,1)}, u32[]{:S(2)}) copy-start(pred[1792,2048]{1,0:T(32,128)(4,1)} %fusion) | copy-start | bytes 11010052
  450.4 1.9 copy-start.2
  463.1 106.1 %reduce-scatter.5.cloned.1.call-start = ((), (), s32[]{:S(2)}) async-start(), calls=%async_computation.11 | async-start | bytes 4718592 | tf_op jit(solution)/shard_map/reduce_scatter | solution.py:198
  463.2 12.4 %copy-start.1 = (bf16[1,64,16,1792]{3,2,1,0:T(8,128)(2,1)S(1)}, bf16[1,64,16,1792]{3,2,1,0:T(8,128)(2,1)}, u32[]{:S(2)}) copy-start(bf16[1,64,16,1792]{3,2,1,0:T(8,128)(2,1)} %get-tuple-element.5) | copy-start | bytes 11010052
  463.2 12.4 %copy-start.7 = (pred[2048,1792]{1,0:T(32,128)(4,1)S(1)}, pred[2048,1792]{1,0:T(32,128)(4,1)}, u32[]{:S(2)}) copy-start(pred[2048,1792]{1,0:T(32,128)(4,1)} %fusion.1) | copy-start | bytes 11010052
  513.7 55.6 %all-to-all-start.2 = ((bf16[4,32,2048]{2,1,0:T(8,128)(2,1)}), bf16[4,32,2048]{2,1,0:T(8,128)(2,1)S(1)}, u32[]{:S(2)}, u32[]{:S(2)}) async-start(bf16[4,32,2048]{2,1,0:T(8,128)(2,1)} %bitcast.62), calls=%async_computation.3 | async-start | bytes 1048576 | tf_op jit(solution)/shard_map/all_to_all | solution.py:199
  569.3 19.8 %all-to-all-start.4 = ((bf16[4,32,2048]{2,1,0:T(8,128)(2,1)}), bf16[4,32,2048]{2,1,0:T(8,128)(2,1)S(1)}, u32[]{:S(2)}, u32[]{:S(2)}) async-start(bf16[4,32,2048]{2,1,0:T(8,128)(2,1)} %bitcast.61), calls=%async_computation.6 | async-start | bytes 1048576 | tf_op jit(solution)/shard_map/all_to_all | solution.py:199
  589.1 18.7 %all-to-all-start.3 = ((bf16[32,8,1024]{2,0,1:T(8,128)(2,1)}), bf16[32,8,1024]{2,0,1:T(8,128)(2,1)S(1)}, u32[]{:S(2)}, u32[]{:S(2)}) async-start(bf16[32,8,1024]{2,0,1:T(8,128)(2,1)} %copy.34), calls=%async_computation.4 | async-start | bytes 1048576 | tf_op jit(solution)/shard_map/all_to_all | solution.py:200
  607.7 17.5 %all-to-all-start.5 = ((bf16[32,8,1024]{2,0,1:T(8,128)(2,1)}), bf16[32,8,1024]{2,0,1:T(8,128)(2,1)S(1)}, u32[]{:S(2)}, u32[]{:S(2)}) async-start(bf16[32,8,1024]{2,0,1:T(8,128)(2,1)} %copy.36), calls=%async_computation.7 | async-start | bytes 1048576 | tf_op jit(solution)/shard_map/all_to_all | solution.py:200
Sparse Core Ops, SparseCore 0:
  85.7 34.6 all-gather.2
  122.9 36.7 all-gather.4
  463.3 50.4 reduce-scatter.2
  517.9 51.3 reduce-scatter.4

commit v3 on v2

--- a/solution.py
+++ b/solution.py
@@ -188,14 +188,15 @@
     up_w = jnp.where(full > 0, up_weight, 0)
     down_w = jnp.where(full_t > 0, down_weight, 0)
 
-    both = jnp.stack([tokens, cotangent])
-    both = lax.all_to_all(both, "col", split_axis=1, concat_axis=2, tiled=True)
-    both = lax.all_to_all(both, "row", split_axis=2, concat_axis=1, tiled=True)
-    toks = lax.all_gather(both[0], "col", axis=0, tiled=True)
-    cots = lax.all_gather(both[1], "col", axis=0, tiled=True)
-
-    def collect(x):
-        x = lax.psum_scatter(x, "col", scatter_dimension=0, tiled=True)
+    def spread(x):
+        x = lax.all_to_all(x, "col", split_axis=0, concat_axis=1, tiled=True)
+        x = lax.all_to_all(x, "row", split_axis=1, concat_axis=0, tiled=True)
+        return lax.all_gather(x, "col", axis=0, tiled=True)
+
+    def col_sum(x):
+        return lax.psum_scatter(x, "col", scatter_dimension=0, tiled=True)
+
+    def home(x):
         x = lax.all_to_all(x, "row", split_axis=0, concat_axis=1, tiled=True)
         return lax.all_to_all(x, "col", split_axis=1, concat_axis=0, tiled=True)
 
@@ -208,14 +209,18 @@
     def tn(a, b):
         return lax.dot_general(a, b, (((0,), (0,)), ((), ())), preferred_element_type=f32)
 
+    toks = spread(tokens)
+    cots = spread(cotangent)
     hidden, gate_cot, up_cot = exchange(
         nn(toks, gate_w).astype(bf16), nn(toks, up_w).astype(bf16), nt(cots, down_w).astype(bf16)
     )
-    output = collect(nn(hidden, down_w).astype(bf16))
+    output = home(col_sum(nn(hidden, down_w).astype(bf16)))
+    in_sum = col_sum((nt(gate_cot, gate_w) + nt(up_cot, up_w)).astype(bf16))
     down_grad = jnp.where(full_t > 0, tn(hidden, cots), 0).astype(bf16)
+    up_grad = jnp.where(full > 0, tn(toks, up_cot), 0).astype(bf16)
     gate_grad = jnp.where(full > 0, tn(toks, gate_cot), 0).astype(bf16)
-    input_grad = collect((nt(gate_cot, gate_w) + nt(up_cot, up_w)).astype(bf16))
-    up_grad = jnp.where(full > 0, tn(toks, up_cot), 0).astype(bf16)
+    in_sum, down_grad, up_grad = lax.optimization_barrier((in_sum, down_grad, up_grad))
+    input_grad = home(in_sum)
     return output, input_grad, gate_grad, up_grad, down_grad
 
 

time: 639 us -> 587 us (0.919)
  waiting for transfers between devices: 114 us -> 73.8 us
  local copies, waits for them, and re-layouts: 43.3 us -> 17.3 us
  blocking collectives: 50.1 us -> 65 us
    all_gather x2, waiting for transfers between devices: 36.9 us -> 4.57 us  [spread(): return lax.all_gather(x, 'col', axis=0, tiled=True)]
    reduce_scatter x2, waiting for transfers between devices: 77.5 us -> 48.3 us  [col_sum(): return lax.psum_scatter(x, 'col', scatter_dimension=0, tiled=True)]
    all_to_all x4, waiting for transfers between devices: 0.01 us -> 20.9 us  [the longest x2 12.9 us: home(): x = lax.all_to_all(x, 'row', split_axis=0, concat_axis=1, tiled=True)]
    all_to_all x2 -> x4, blocking collectives: 50.1 us -> 65 us  [the longest x2 34.4 us: spread(): x = lax.all_to_all(x, 'row', split_axis=1, concat_axis=0, tiled=True)]
    all_to_all x9 -> x12, local copies, waits for them, and re-layouts: 18.4 us -> 5.19 us  [the longest x4 2.41 us: home(): return lax.all_to_all(x, 'col', split_axis=1, concat_axis=0, tiled=True)]
    unnamed x24 -> x28, local copies, waits for them, and re-layouts: 14 us -> 5.01 us
  transfers between devices with their start and end apart: 8 -> 8, of which waited for: 4 -> 5; matrix products, arithmetic and copies ran while one was open for 16% -> 18% of each run, Pallas kernels for 0% -> 0%
where the time goes in v3:
time: 587 us; the launch traced here: 583 us
  Pallas kernels  269 us (46%)
  matrix products  127 us (22%)
  waiting for transfers between devices  73.8 us (13%)
  blocking collectives  65 us (11%)
  local copies, waits for them, and re-layouts  17.3 us (3%)
  starting transfers between devices  17.1 us (3%)
  between operations  14.2 us (2%)
    pallas_call x1, Pallas kernels, exchange(): pl.pallas_call(functools.partial(exchange_kernel, count, chunks), out_sha...  269 us
    reduce_scatter x2, waiting for transfers between devices, col_sum(): return lax.psum_scatter(x, 'col', scatter_dimension=0, tiled=True)  48.3 us
    dot_general x3, matrix products, tn(): lax.dot_general(a, b, (((0,), (0,)), ((), ())), preferred_element_type=f32)  40.4 us
    dot_general x3, matrix products, nt(): lax.dot_general(a, b, (((1,), (1,)), ((), ())), preferred_element_type=f32)  40.1 us
    dot_general x3, matrix products, nn(): lax.dot_general(a, b, (((1,), (0,)), ((), ())), preferred_element_type=f32)  37 us
    all_to_all x2, blocking collectives, spread(): x = lax.all_to_all(x, 'row', split_axis=1, concat_axis=0, tiled=True)  34.4 us
    all_to_all x2, blocking collectives, spread(): x = lax.all_to_all(x, 'col', split_axis=0, concat_axis=1, tiled=True)  30.5 us
    all_to_all x2, waiting for transfers between devices, home(): x = lax.all_to_all(x, 'row', split_axis=0, concat_axis=1, tiled=True)  12.9 us
  transfers between devices with their start and end apart: 8, of which 5 were waited for; matrix products, arithmetic and copies ran while one was open for 18% of the time, Pallas kernels for 0%

profile of v3, /device:TPU:0, one launch (start us, length us, event | category | flops | bytes accessed | tf_op | source)
XLA Modules:
  0.0 583.1 jit_solution(18068377358569996429)
XLA Ops:
  7.2 0.0 copy-start.3
  7.2 0.0 all-gather.3.cloned.1.call-start
  7.2 15.1 %all_to_all.140 = bf16[8,32,1024]{2,1,0:T(8,128)(2,1)S(1)} all-to-all(bf16[8,32,1024]{2,1,0:T(8,128)(2,1)} %bitcast.69), channel_id=1, replica_groups=mesh['row'=4,'col'=8] {'col'}, dimensions={0} | all-to-all | bytes 1048576 | tf_op jit(solution)/shard_map/all_to_all | solution.py:192
  22.3 0.3 copy.31
  22.6 0.4 all_to_all.107
  23.0 0.0 copy-start.5
  23.0 0.3 copy.32
  23.3 18.6 %all_to_all.141 = bf16[32,4,2048]{2,0,1:T(8,128)(2,1)} all-to-all(bf16[32,4,2048]{2,0,1:T(8,128)(2,1)S(1)} %copy.32), channel_id=1, replica_groups=mesh['row'=4,'col'=8] {'row'}, dimensions={1} | all-to-all | bytes 1048576 | tf_op jit(solution)/shard_map/all_to_all | solution.py:193
  41.9 0.0 all-gather.3.cloned.1.call-update
  41.9 0.0 all-gather.5.cloned.1.call-start
  42.0 0.0 copy-done.3
  42.0 15.5 %all_to_all.142 = bf16[8,32,1024]{2,1,0:T(8,128)(2,1)S(1)} all-to-all(bf16[8,32,1024]{2,1,0:T(8,128)(2,1)S(1)} %bitcast.70), channel_id=1, replica_groups=mesh['row'=4,'col'=8] {'col'}, dimensions={0} | all-to-all | bytes 1048576 | tf_op jit(solution)/shard_map/all_to_all | solution.py:192
  57.5 0.3 copy.33
  57.8 0.4 all_to_all.114
  58.2 0.3 copy.34
  58.5 15.8 %all_to_all.143 = bf16[32,4,2048]{2,0,1:T(8,128)(2,1)} all-to-all(bf16[32,4,2048]{2,0,1:T(8,128)(2,1)S(1)} %copy.34), channel_id=1, replica_groups=mesh['row'=4,'col'=8] {'row'}, dimensions={1} | all-to-all | bytes 1048576 | tf_op jit(solution)/shard_map/all_to_all | solution.py:193
  74.3 0.0 all-gather.5.cloned.1.call-update
  74.3 0.6 reduce-scatter.3.cloned.1.call-start
  74.9 0.0 copy-done.5
  74.9 5.3 fusion.2
  80.2 3.9 fusion.3
  84.1 14.7 %convolution_convert_fusion.3 = bf16[1792,1024]{0,1:T(8,128)(2,1)} fusion(bf16[1024,2048]{1,0:T(8,128)(2,1)} %all-gather.3.cloned.1.call-done, pred[2048,1792]{1,0:T(32,128)(4,1)} %fusion.3, bf16[2048,1792]{1,0:T(8,128)(2,1)} %param.8), kind=kOutput, calls=%fused_computation.11 | convolution fusion | flops 7521697792 | bytes 18874368 | tf_op jit(solution)/shard_map/dot_general | solution.py:204
  98.8 0.0 copy-done.4
  98.8 0.0 copy-done.7
  98.8 12.9 %convolution_convert_fusion.2 = bf16[1792,1024]{0,1:T(8,128)(2,1)} fusion(bf16[1024,2048]{1,0:T(8,128)(2,1)S(1)} %copy-done.4, pred[2048,1792]{1,0:T(32,128)(4,1)S(1)} %copy-done.7, bf16[2048,1792]{1,0:T(8,128)(2,1)} %param.9), kind=kOutput, calls=%fused_computation.10 | convolution fusion | flops 7521697792 | bytes 18874368 | tf_op jit(solution)/shard_map/dot_general | solution.py:204
  111.7 4.6 all-gather.5.cloned.1.call-done
  116.3 14.4 %convolution_convert_fusion.5 = bf16[1792,1024]{0,1:T(8,128)(2,1)} fusion(bf16[1024,2048]{1,0:T(8,128)(2,1)} %all-gather.5.cloned.1.call-done, pred[1792,2048]{1,0:T(32,128)(4,1)} %fusion.2, bf16[1792,2048]{1,0:T(8,128)(2,1)} %param.10), kind=kOutput, calls=%fused_computation.13 | convolution fusion | flops 7521697792 | bytes 18874368 | tf_op jit(solution)/shard_map/dot_general | solution.py:207
  130.6 0.0 copy-done
  130.7 269.0 %shard_map.101 = bf16[3,64,16,1792]{3,2,1,0:T(8,128)(2,1)} custom-call(bf16[64,16,1792]{2,1,0:T(8,128)(2,1)S(1)} %bitcast.52, bf16[64,16,1792]{2,1,0:T(8,128)(2,1)} %bitcast.59, bf16[64,16,1792]{2,1,0:T(8,128)(2,1)} %bitcast.60), custom_call_target="tpu_custom_call" | custom-call | flops 73400320 | bytes 22020096 | tf_op jit(solution)/shard_map/pallas_call | solution.py:144
  399.6 0.0 slice-start.1
  399.6 0.0 copy-start.6
  399.6 7.1 %fusion.23 = (bf16[1,64,16,1792]{3,2,1,0:T(8,128)(2,1)}, bf16[1,64,16,1792]{3,2,1,0:T(8,128)(2,1)}, bf16[1,64,16,1792]{3,2,1,0:T(8,128)(2,1)S(1)}) fusion(bf16[3,64,16,1792]{3,2,1,0:T(8,128)(2,1)} %shard_map.101), kind=kLoop, calls=%fused_computation.47 | loop fusion | bytes 22020096 | tf_op jit(solution)/shard_map/slice | solution.py:158
  406.8 1.9 copy-done.2
  408.7 0.0 slice-done
  408.7 0.0 slice-done.1
  408.7 1.5 copy-done.6
  410.1 9.4 %convolution_convert_fusion.4 = bf16[1024,2048]{1,0:T(8,128)(2,1)} fusion(bf16[1024,1792]{1,0:T(8,128)(2,1)S(1)} %bitcast.57, pred[1792,2048]{1,0:T(32,128)(4,1)S(1)} %copy-done.6, bf16[1792,2048]{1,0:T(8,128)(2,1)S(1)} %bitcast.74), kind=kOutput, calls=%fused_computation.12 | convolution fusion | flops 7521959936 | bytes 18874368 | tf_op jit(solution)/shard_map/dot_general | solution.py:204
  419.5 0.0 reduce-scatter.3.cloned.1.call-update
  419.6 0.0 reduce-scatter.5.cloned.1.call-start
  419.6 0.0 slice-start.3
  419.6 14.2 %fusion.4 = f32[1024,2048]{1,0:T(8,128)} fusion(bf16[1024,1792]{1,0:T(8,128)(2,1)} %bitcast.53, pred[2048,1792]{1,0:T(32,128)(4,1)} %fusion.3, bf16[2048,1792]{1,0:T(8,128)(2,1)} %param.8), kind=kOutput, calls=%fused_computation.17 | convolution fusion | flops 7519862784 | bytes 23068672 | tf_op jit(solution)/shard_map/dot_general | solution.py:207
  433.9 11.5 %add_convert_fusion = bf16[1024,2048]{1,0:T(8,128)(2,1)} fusion(f32[1024,2048]{1,0:T(8,128)} %fusion.4, bf16[1024,1792]{1,0:T(8,128)(2,1)S(1)} %bitcast.56, pred[2048,1792]{1,0:T(32,128)(4,1)S(1)} %copy-done.8, bf16[2048,1792]{1,0:T(8,128)(2,1)S(1)} %bitcast.76), kind=kOutput, calls=%fused_computation.5 | convolution fusion | flops 7524057088 | bytes 27262976 | tf_op jit(solution)/shard_map/dot_general | solution.py:207
  445.4 0.0 reduce-scatter.5.cloned.1.call-update
  445.4 13.7 %select_convert_fusion = bf16[1792,2048]{1,0:T(8,128)(2,1)} fusion(pred[1792,2048]{1,0:T(32,128)(4,1)} %fusion.2, bf16[1024,1792]{1,0:T(8,128)(2,1)} %bitcast.58, bf16[1024,2048]{1,0:T(8,128)(2,1)} %all-gather.5.cloned.1.call-done), kind=kOutput, calls=%fused_computation.4 | convolution fusion | flops 7523532800 | bytes 18874368 | tf_op jit(solution)/shard_map/dot_general | solution.py:210
  459.1 11.0 %reduce-scatter.3.cloned.1.call-done = bf16[128,2048]{1,0:T(8,128)(2,1)} async-done(((bf16[1024,2048]{1,0:T(8,128)(2,1)}), bf16[128,2048]{1,0:T(8,128)(2,1)}) %reduce-scatter.3.cloned.1.call-update) | async-done | bytes 524304 | tf_op jit(solution)/shard_map/reduce_scatter | solution.py:197
  470.1 4.9 all-to-all-start.4
  474.9 13.4 %fusion.1 = bf16[2048,1792]{1,0:T(8,128)(2,1)} fusion(pred[2048,1792]{1,0:T(32,128)(4,1)} %fusion.3, bf16[1024,1792]{1,0:T(8,128)(2,1)} %bitcast.55, bf16[1024,2048]{1,0:T(8,128)(2,1)} %all-gather.3.cloned.1.call-done), kind=kOutput, calls=%fused_computation.3 | convolution fusion | flops 7523532800 | bytes 18874368 | tf_op jit(solution)/shard_map/dot_general | solution.py:210
  488.3 37.3 %reduce-scatter.5.cloned.1.call-done = bf16[128,2048]{1,0:T(8,128)(2,1)} async-done(((bf16[1024,2048]{1,0:T(8,128)(2,1)}), bf16[128,2048]{1,0:T(8,128)(2,1)}) %reduce-scatter.5.cloned.1.call-update) | async-done | bytes 524304 | tf_op jit(solution)/shard_map/reduce_scatter | solution.py:197
  525.6 0.0 all-to-all-done.4
  525.6 4.6 all-to-all-start.6
  530.2 0.4 copy.35
  530.6 0.1 all_to_all.121
  530.7 1.1 copy.36
  531.8 12.9 %all-to-all-done.6 = bf16[4,32,2048]{2,1,0:T(8,128)(2,1)S(1)} async-done(((bf16[4,32,2048]{2,1,0:T(8,128)(2,1)}), bf16[4,32,2048]{2,1,0:T(8,128)(2,1)S(1)}, u32[]{:S(2)}, u32[]{:S(2)}) %all-to-all-start.6) | async-done | bytes 524320 | tf_op jit(solution)/shard_map/all_to_all | solution.py:200
  544.7 3.5 all-to-all-start.5
  548.2 0.4 copy.38
  548.6 0.1 all_to_all.128
  548.7 1.1 copy.39
  549.8 8.0 %all-to-all-done.5 = bf16[32,8,1024]{2,0,1:T(8,128)(2,1)S(1)} async-done(((bf16[32,8,1024]{2,0,1:T(8,128)(2,1)}), bf16[32,8,1024]{2,0,1:T(8,128)(2,1)S(1)}, u32[]{:S(2)}, u32[]{:S(2)}) %all-to-all-start.5) | async-done | bytes 524320 | tf_op jit(solution)/shard_map/all_to_all | solution.py:201
  557.9 3.5 all-to-all-start.7
  561.4 13.4 %fusion = bf16[2048,1792]{1,0:T(8,128)(2,1)} fusion(pred[2048,1792]{1,0:T(32,128)(4,1)} %fusion.3, bf16[1024,1792]{1,0:T(8,128)(2,1)} %bitcast.54, bf16[1024,2048]{1,0:T(8,128)(2,1)} %all-gather.3.cloned.1.call-done), kind=kOutput, calls=%fused_computation.1 | convolution fusion | flops 7523532800 | bytes 18874368 | tf_op jit(solution)/shard_map/dot_general | solution.py:210
  574.7 0.0 all-to-all-done.7
  574.7 0.8 copy.56
  575.5 0.8 copy.57
  (17 shorter events, 0.0 us)
Async XLA Ops:
  7.2 34.8 %copy-start.3 = (bf16[256,1024]{1,0:T(8,128)(2,1)S(1)}, bf16[256,1024]{1,0:T(8,128)(2,1)}, u32[]{:S(2)}) copy-start(bf16[256,1024]{1,0:T(8,128)(2,1)} %param.7) | copy-start | bytes 1572868
  7.2 76.9 %all-gather.3.cloned.1.call-start = ((), (), s32[]{:S(2)}) async-start(), calls=%async_computation.10 | async-start | bytes 4718592 | tf_op jit(solution)/shard_map/all_gather | solution.py:194
  23.0 51.9 %copy-start.5 = (s32[64,112]{1,0:T(8,128)S(1)}, s32[64,112]{1,0:T(8,128)}, u32[]{:S(2)}) copy-start(s32[64,112]{1,0:T(8,128)} %param.11) | copy-start | bytes 86020
  41.9 74.4 %all-gather.5.cloned.1.call-start = ((), (), s32[]{:S(2)}) async-start(), calls=%async_computation.11 | async-start | bytes 4718592 | tf_op jit(solution)/shard_map/all_gather | solution.py:194
  74.3 395.8 %reduce-scatter.3.cloned.1.call-start = ((), (), s32[]{:S(2)}) async-start(), calls=%async_computation.12 | async-start | bytes 4718592 | tf_op jit(solution)/shard_map/reduce_scatter | solution.py:197
  84.1 14.7 %copy-start.4 = (bf16[1024,2048]{1,0:T(8,128)(2,1)S(1)}, bf16[1024,2048]{1,0:T(8,128)(2,1)}, u32[]{:S(2)}) copy-start(bf16[1024,2048]{1,0:T(8,128)(2,1)} %all-gather.3.cloned.1.call-done) | copy-start | bytes 12582916
  84.1 14.7 %copy-start.7 = (pred[2048,1792]{1,0:T(32,128)(4,1)S(1)}, pred[2048,1792]{1,0:T(32,128)(4,1)}, u32[]{:S(2)}) copy-start(pred[2048,1792]{1,0:T(32,128)(4,1)} %fusion.3) | copy-start | bytes 11010052
  116.3 14.4 %copy-start = (bf16[1792,1024]{0,1:T(8,128)(2,1)S(1)}, bf16[1792,1024]{0,1:T(8,128)(2,1)}, u32[]{:S(2)}) copy-start(bf16[1792,1024]{0,1:T(8,128)(2,1)} %convolution_convert_fusion.3) | copy-start | bytes 11010052
  130.7 278.0 %slice-start = ((s8[7340032]{0:T(1024)(128)(4,1)}), s8[3145728]{0:T(1024)(128)(4,1)S(1)}, s32[]{:S(2)}) async-start(s8[7340032]{0:T(1024)(128)(4,1)} %bitcast.73), calls=%async_computation.14 | async-start | bytes 6291456
  399.6 9.0 %slice-start.1 = ((s8[7340032]{0:T(1024)(128)(4,1)}), s8[4194304]{0:T(1024)(128)(4,1)S(1)}, s32[]{:S(2)}) async-start(s8[7340032]{0:T(1024)(128)(4,1)} %bitcast.73), calls=%async_computation.15 | async-start | bytes 8388608
  399.6 10.5 %copy-start.6 = (pred[1792,2048]{1,0:T(32,128)(4,1)S(1)}, pred[1792,2048]{1,0:T(32,128)(4,1)}, u32[]{:S(2)}) copy-start(pred[1792,2048]{1,0:T(32,128)(4,1)} %fusion.2) | copy-start | bytes 11010052
  406.8 1.9 copy-start.2
  419.5 14.3 %slice-start.2 = ((s8[7340032]{0:T(1024)(128)(4,1)}), s8[3145728]{0:T(1024)(128)(4,1)S(1)}, s32[]{:S(2)}) async-start(s8[7340032]{0:T(1024)(128)(4,1)} %bitcast.75), calls=%async_computation.16 | async-start | bytes 6291456
  419.6 106.0 %reduce-scatter.5.cloned.1.call-start = ((), (), s32[]{:S(2)}) async-start(), calls=%async_computation.13 | async-start | bytes 4718592 | tf_op jit(solution)/shard_map/reduce_scatter | solution.py:197
  419.6 14.2 %copy-start.1 = (bf16[1,64,16,1792]{3,2,1,0:T(8,128)(2,1)S(1)}, bf16[1,64,16,1792]{3,2,1,0:T(8,128)(2,1)}, u32[]{:S(2)}) copy-start(bf16[1,64,16,1792]{3,2,1,0:T(8,128)(2,1)} %get-tuple-element.11) | copy-start | bytes 11010052
  419.6 14.2 %slice-start.3 = ((s8[7340032]{0:T(1024)(128)(4,1)}), s8[4194304]{0:T(1024)(128)(4,1)S(1)}, s32[]{:S(2)}) async-start(s8[7340032]{0:T(1024)(128)(4,1)} %bitcast.75), calls=%async_computation.17 | async-start | bytes 8388608
  419.6 14.2 %copy-start.8 = (pred[2048,1792]{1,0:T(32,128)(4,1)S(1)}, pred[2048,1792]{1,0:T(32,128)(4,1)}, u32[]{:S(2)}) copy-start(pred[2048,1792]{1,0:T(32,128)(4,1)} %fusion.3) | copy-start | bytes 11010052
  470.1 55.5 %all-to-all-start.4 = ((bf16[4,32,2048]{2,1,0:T(8,128)(2,1)}), bf16[4,32,2048]{2,1,0:T(8,128)(2,1)S(1)}, u32[]{:S(2)}, u32[]{:S(2)}) async-start(bf16[4,32,2048]{2,1,0:T(8,128)(2,1)} %bitcast.72), calls=%async_computation.5 | async-start | bytes 1048576 | tf_op jit(solution)/shard_map/all_to_all | solution.py:200
  525.6 19.1 %all-to-all-start.6 = ((bf16[4,32,2048]{2,1,0:T(8,128)(2,1)}), bf16[4,32,2048]{2,1,0:T(8,128)(2,1)S(1)}, u32[]{:S(2)}, u32[]{:S(2)}) async-start(bf16[4,32,2048]{2,1,0:T(8,128)(2,1)} %bitcast.71), calls=%async_computation.8 | async-start | bytes 1048576 | tf_op jit(solution)/shard_map/all_to_all | solution.py:200
  544.7 13.2 %all-to-all-start.5 = ((bf16[32,8,1024]{2,0,1:T(8,128)(2,1)}), bf16[32,8,1024]{2,0,1:T(8,128)(2,1)S(1)}, u32[]{:S(2)}, u32[]{:S(2)}) async-start(bf16[32,8,1024]{2,0,1:T(8,128)(2,1)} %copy.36), calls=%async_computation.6 | async-start | bytes 1048576 | tf_op jit(solution)/shard_map/all_to_all | solution.py:201
  557.9 16.9 %all-to-all-start.7 = ((bf16[32,8,1024]{2,0,1:T(8,128)(2,1)}), bf16[32,8,1024]{2,0,1:T(8,128)(2,1)S(1)}, u32[]{:S(2)}, u32[]{:S(2)}) async-start(bf16[32,8,1024]{2,0,1:T(8,128)(2,1)} %copy.39), calls=%async_computation.9 | async-start | bytes 1048576 | tf_op jit(solution)/shard_map/all_to_all | solution.py:201
Sparse Core Ops, SparseCore 0:
  42.0 35.5 all-gather.2
  79.5 36.7 all-gather.4
  419.7 50.3 reduce-scatter.2
  474.2 51.3 reduce-scatter.4

commit v4 on v3

--- a/solution.py
+++ b/solution.py
@@ -219,7 +219,9 @@
     down_grad = jnp.where(full_t > 0, tn(hidden, cots), 0).astype(bf16)
     up_grad = jnp.where(full > 0, tn(toks, up_cot), 0).astype(bf16)
     gate_grad = jnp.where(full > 0, tn(toks, gate_cot), 0).astype(bf16)
-    in_sum, down_grad, up_grad = lax.optimization_barrier((in_sum, down_grad, up_grad))
+    in_sum, output, down_grad, up_grad = lax.optimization_barrier(
+        (in_sum, output, down_grad, up_grad)
+    )
     input_grad = home(in_sum)
     return output, input_grad, gate_grad, up_grad, down_grad
 

time: 587 us -> 579 us (0.986)
  waiting for transfers between devices: 73.8 us -> 51.3 us
  blocking collectives: 65 us -> 84 us
    all_to_all x0 -> x1, blocking collectives: none -> 19.1 us  [home(): x = lax.all_to_all(x, 'row', split_axis=0, concat_axis=1, tiled=True)]
    all_to_all x2 -> x1, waiting for transfers between devices: 12.9 us -> 0.9 us  [home(): x = lax.all_to_all(x, 'row', split_axis=0, concat_axis=1, tiled=True)]
    all_to_all x2, waiting for transfers between devices: 8.05 us -> 0.01 us  [home(): return lax.all_to_all(x, 'col', split_axis=1, concat_axis=0, tiled=True)]
  transfers between devices with their start and end apart: 8 -> 7, of which waited for: 5 -> 4; matrix products, arithmetic and copies ran while one was open for 18% -> 18% of each run, Pallas kernels for 0% -> 0%
where the time goes in v4:
time: 579 us; the launch traced here: 576 us
  Pallas kernels  269 us (46%)
  matrix products  127 us (22%)
  blocking collectives  84 us (15%)
  waiting for transfers between devices  51.3 us (9%)
  local copies, waits for them, and re-layouts  17.3 us (3%)
  between operations  14.2 us (2%)
  starting transfers between devices  12.5 us (2%)
    pallas_call x1, Pallas kernels, exchange(): pl.pallas_call(functools.partial(exchange_kernel, count, chunks), out_sha...  269 us
    reduce_scatter x2, waiting for transfers between devices, col_sum(): return lax.psum_scatter(x, 'col', scatter_dimension=0, tiled=True)  45.9 us
    dot_general x3, matrix products, tn(): lax.dot_general(a, b, (((0,), (0,)), ((), ())), preferred_element_type=f32)  41 us
    dot_general x3, matrix products, nt(): lax.dot_general(a, b, (((1,), (1,)), ((), ())), preferred_element_type=f32)  40.1 us
    dot_general x3, matrix products, nn(): lax.dot_general(a, b, (((1,), (0,)), ((), ())), preferred_element_type=f32)  37.1 us
    all_to_all x2, blocking collectives, spread(): x = lax.all_to_all(x, 'row', split_axis=1, concat_axis=0, tiled=True)  34.4 us
    all_to_all x2, blocking collectives, spread(): x = lax.all_to_all(x, 'col', split_axis=0, concat_axis=1, tiled=True)  30.5 us
    all_to_all x1, blocking collectives, home(): x = lax.all_to_all(x, 'row', split_axis=0, concat_axis=1, tiled=True)  19.1 us
  transfers between devices with their start and end apart: 7, of which 4 were waited for; matrix products, arithmetic and copies ran while one was open for 18% of the time, Pallas kernels for 0%

profile of v4, /device:TPU:0, one launch (start us, length us, event | category | flops | bytes accessed | tf_op | source)
XLA Modules:
  0.0 575.9 jit_solution(11021877198929347003)
XLA Ops:
  7.2 0.0 copy-start.3
  7.2 0.0 all-gather.3.cloned.1.call-start
  7.2 15.1 %all_to_all.140 = bf16[8,32,1024]{2,1,0:T(8,128)(2,1)S(1)} all-to-all(bf16[8,32,1024]{2,1,0:T(8,128)(2,1)} %bitcast.69), channel_id=1, replica_groups=mesh['row'=4,'col'=8] {'col'}, dimensions={0} | all-to-all | bytes 1048576 | tf_op jit(solution)/shard_map/all_to_all | solution.py:192
  22.3 0.3 copy.31
  22.6 0.4 all_to_all.107
  23.0 0.0 copy-start.5
  23.0 0.3 copy.32
  23.3 18.6 %all_to_all.141 = bf16[32,4,2048]{2,0,1:T(8,128)(2,1)} all-to-all(bf16[32,4,2048]{2,0,1:T(8,128)(2,1)S(1)} %copy.32), channel_id=1, replica_groups=mesh['row'=4,'col'=8] {'row'}, dimensions={1} | all-to-all | bytes 1048576 | tf_op jit(solution)/shard_map/all_to_all | solution.py:193
  41.9 0.0 all-gather.3.cloned.1.call-update
  41.9 0.0 all-gather.5.cloned.1.call-start
  42.0 0.0 copy-done.3
  42.0 15.5 %all_to_all.142 = bf16[8,32,1024]{2,1,0:T(8,128)(2,1)S(1)} all-to-all(bf16[8,32,1024]{2,1,0:T(8,128)(2,1)S(1)} %bitcast.70), channel_id=1, replica_groups=mesh['row'=4,'col'=8] {'col'}, dimensions={0} | all-to-all | bytes 1048576 | tf_op jit(solution)/shard_map/all_to_all | solution.py:192
  57.5 0.3 copy.33
  57.8 0.4 all_to_all.114
  58.2 0.3 copy.34
  58.5 15.8 %all_to_all.143 = bf16[32,4,2048]{2,0,1:T(8,128)(2,1)} all-to-all(bf16[32,4,2048]{2,0,1:T(8,128)(2,1)S(1)} %copy.34), channel_id=1, replica_groups=mesh['row'=4,'col'=8] {'row'}, dimensions={1} | all-to-all | bytes 1048576 | tf_op jit(solution)/shard_map/all_to_all | solution.py:193
  74.3 0.0 all-gather.5.cloned.1.call-update
  74.3 0.6 reduce-scatter.5.cloned.1.call-start
  74.9 0.0 copy-done.5
  74.9 5.4 fusion.2
  80.3 3.9 fusion.3
  84.2 14.7 %convolution_convert_fusion.3 = bf16[1792,1024]{0,1:T(8,128)(2,1)} fusion(bf16[1024,2048]{1,0:T(8,128)(2,1)} %all-gather.3.cloned.1.call-done, pred[2048,1792]{1,0:T(32,128)(4,1)} %fusion.3, bf16[2048,1792]{1,0:T(8,128)(2,1)} %param.8), kind=kOutput, calls=%fused_computation.11 | convolution fusion | flops 7521697792 | bytes 18874368 | tf_op jit(solution)/shard_map/dot_general | solution.py:204
  98.9 0.0 copy-done.4
  98.9 0.0 copy-done.7
  98.9 13.0 %convolution_convert_fusion.2 = bf16[1792,1024]{0,1:T(8,128)(2,1)} fusion(bf16[1024,2048]{1,0:T(8,128)(2,1)S(1)} %copy-done.4, pred[2048,1792]{1,0:T(32,128)(4,1)S(1)} %copy-done.7, bf16[2048,1792]{1,0:T(8,128)(2,1)} %param.9), kind=kOutput, calls=%fused_computation.10 | convolution fusion | flops 7521697792 | bytes 18874368 | tf_op jit(solution)/shard_map/dot_general | solution.py:204
  111.9 4.4 all-gather.5.cloned.1.call-done
  116.3 14.4 %convolution_convert_fusion.5 = bf16[1792,1024]{0,1:T(8,128)(2,1)} fusion(bf16[1024,2048]{1,0:T(8,128)(2,1)} %all-gather.5.cloned.1.call-done, pred[1792,2048]{1,0:T(32,128)(4,1)} %fusion.2, bf16[1792,2048]{1,0:T(8,128)(2,1)} %param.10), kind=kOutput, calls=%fused_computation.13 | convolution fusion | flops 7521697792 | bytes 18874368 | tf_op jit(solution)/shard_map/dot_general | solution.py:207
  130.6 0.0 copy-done
  130.6 269.1 %shard_map.101 = bf16[3,64,16,1792]{3,2,1,0:T(8,128)(2,1)} custom-call(bf16[64,16,1792]{2,1,0:T(8,128)(2,1)S(1)} %bitcast.52, bf16[64,16,1792]{2,1,0:T(8,128)(2,1)} %bitcast.59, bf16[64,16,1792]{2,1,0:T(8,128)(2,1)} %bitcast.60), custom_call_target="tpu_custom_call" | custom-call | flops 73400320 | bytes 22020096 | tf_op jit(solution)/shard_map/pallas_call | solution.py:144
  399.8 0.0 slice-start.1
  399.8 0.0 copy-start.6
  399.8 7.1 %fusion.23 = (bf16[1,64,16,1792]{3,2,1,0:T(8,128)(2,1)S(1)}, bf16[1,64,16,1792]{3,2,1,0:T(8,128)(2,1)}, bf16[1,64,16,1792]{3,2,1,0:T(8,128)(2,1)}) fusion(bf16[3,64,16,1792]{3,2,1,0:T(8,128)(2,1)} %shard_map.101), kind=kLoop, calls=%fused_computation.47 | loop fusion | bytes 22020096 | tf_op jit(solution)/shard_map/slice | solution.py:158
  406.9 1.9 copy-done.2
  408.8 0.0 slice-done
  408.8 1.5 copy-done.6
  410.3 9.4 %convolution_convert_fusion.4 = bf16[1024,2048]{1,0:T(8,128)(2,1)} fusion(bf16[1024,1792]{1,0:T(8,128)(2,1)S(1)} %bitcast.57, pred[1792,2048]{1,0:T(32,128)(4,1)S(1)} %copy-done.6, bf16[1792,2048]{1,0:T(8,128)(2,1)S(1)} %bitcast.74), kind=kOutput, calls=%fused_computation.12 | convolution fusion | flops 7521959936 | bytes 18874368 | tf_op jit(solution)/shard_map/dot_general | solution.py:204
  419.7 0.0 reduce-scatter.5.cloned.1.call-update
  419.7 0.0 reduce-scatter.3.cloned.1.call-start
  419.8 0.0 slice-start.3
  419.8 14.2 %fusion.4 = f32[1024,2048]{1,0:T(8,128)} fusion(bf16[1024,1792]{1,0:T(8,128)(2,1)} %bitcast.53, pred[2048,1792]{1,0:T(32,128)(4,1)} %fusion.3, bf16[2048,1792]{1,0:T(8,128)(2,1)} %param.8), kind=kOutput, calls=%fused_computation.17 | convolution fusion | flops 7519862784 | bytes 23068672 | tf_op jit(solution)/shard_map/dot_general | solution.py:207
  434.0 0.0 slice-done.3
  434.0 0.0 copy-done.8
  434.0 11.5 %add_convert_fusion = bf16[1024,2048]{1,0:T(8,128)(2,1)} fusion(f32[1024,2048]{1,0:T(8,128)} %fusion.4, bf16[1024,1792]{1,0:T(8,128)(2,1)S(1)} %bitcast.56, pred[2048,1792]{1,0:T(32,128)(4,1)S(1)} %copy-done.8, bf16[2048,1792]{1,0:T(8,128)(2,1)S(1)} %bitcast.76), kind=kOutput, calls=%fused_computation.5 | convolution fusion | flops 7524057088 | bytes 27262976 | tf_op jit(solution)/shard_map/dot_general | solution.py:207
  445.5 0.0 reduce-scatter.3.cloned.1.call-update
  445.5 24.7 %reduce-scatter.5.cloned.1.call-done = bf16[128,2048]{1,0:T(8,128)(2,1)} async-done(((bf16[1024,2048]{1,0:T(8,128)(2,1)}), bf16[128,2048]{1,0:T(8,128)(2,1)}) %reduce-scatter.5.cloned.1.call-update) | async-done | bytes 524304 | tf_op jit(solution)/shard_map/reduce_scatter | solution.py:197
  470.2 4.6 all-to-all-start.4
  474.9 13.6 %select_convert_fusion = bf16[1792,2048]{1,0:T(8,128)(2,1)} fusion(pred[1792,2048]{1,0:T(32,128)(4,1)} %fusion.2, bf16[1024,1792]{1,0:T(8,128)(2,1)} %bitcast.58, bf16[1024,2048]{1,0:T(8,128)(2,1)} %all-gather.5.cloned.1.call-done), kind=kOutput, calls=%fused_computation.4 | convolution fusion | flops 7523532800 | bytes 18874368 | tf_op jit(solution)/shard_map/dot_general | solution.py:210
  488.4 0.9 all-to-all-done.4
  489.3 0.4 copy.35
  489.7 0.1 all_to_all.121
  489.9 1.1 copy.36
  491.0 3.7 all-to-all-start.5
  494.7 14.1 %fusion.1 = bf16[2048,1792]{1,0:T(8,128)(2,1)} fusion(pred[2048,1792]{1,0:T(32,128)(4,1)} %fusion.3, bf16[1024,1792]{1,0:T(8,128)(2,1)} %bitcast.55, bf16[1024,2048]{1,0:T(8,128)(2,1)} %all-gather.3.cloned.1.call-done), kind=kOutput, calls=%fused_computation.3 | convolution fusion | flops 7523532800 | bytes 18874368 | tf_op jit(solution)/shard_map/dot_general | solution.py:210
  508.8 21.2 %reduce-scatter.3.cloned.1.call-done = bf16[128,2048]{1,0:T(8,128)(2,1)} async-done(((bf16[1024,2048]{1,0:T(8,128)(2,1)}), bf16[128,2048]{1,0:T(8,128)(2,1)}) %reduce-scatter.3.cloned.1.call-update) | async-done | bytes 524304 | tf_op jit(solution)/shard_map/reduce_scatter | solution.py:197
  530.0 0.0 all-to-all-done.5
  530.0 19.1 %all_to_all.144 = bf16[4,32,2048]{2,1,0:T(8,128)(2,1)S(1)} all-to-all(bf16[4,32,2048]{2,1,0:T(8,128)(2,1)} %bitcast.71), channel_id=1, replica_groups=mesh['row'=4,'col'=8] {'row'}, dimensions={0} | all-to-all | bytes 1048576 | tf_op jit(solution)/shard_map/all_to_all | solution.py:200
  549.1 0.4 copy.38
  549.5 0.1 all_to_all.128
  549.6 1.1 copy.39
  550.7 3.5 all-to-all-start.7
  554.2 13.4 %fusion = bf16[2048,1792]{1,0:T(8,128)(2,1)} fusion(pred[2048,1792]{1,0:T(32,128)(4,1)} %fusion.3, bf16[1024,1792]{1,0:T(8,128)(2,1)} %bitcast.54, bf16[1024,2048]{1,0:T(8,128)(2,1)} %all-gather.3.cloned.1.call-done), kind=kOutput, calls=%fused_computation.1 | convolution fusion | flops 7523532800 | bytes 18874368 | tf_op jit(solution)/shard_map/dot_general | solution.py:210
  567.5 0.0 all-to-all-done.7
  567.6 0.8 copy.56
  568.3 0.8 copy.57
  (16 shorter events, 0.0 us)
Async XLA Ops:
  7.2 34.8 %copy-start.3 = (bf16[256,1024]{1,0:T(8,128)(2,1)S(1)}, bf16[256,1024]{1,0:T(8,128)(2,1)}, u32[]{:S(2)}) copy-start(bf16[256,1024]{1,0:T(8,128)(2,1)} %param.7) | copy-start | bytes 1572868
  7.2 77.0 %all-gather.3.cloned.1.call-start = ((), (), s32[]{:S(2)}) async-start(), calls=%async_computation.10 | async-start | bytes 4718592 | tf_op jit(solution)/shard_map/all_gather | solution.py:194
  23.0 51.9 %copy-start.5 = (s32[64,112]{1,0:T(8,128)S(1)}, s32[64,112]{1,0:T(8,128)}, u32[]{:S(2)}) copy-start(s32[64,112]{1,0:T(8,128)} %param.11) | copy-start | bytes 86020
  41.9 74.3 %all-gather.5.cloned.1.call-start = ((), (), s32[]{:S(2)}) async-start(), calls=%async_computation.11 | async-start | bytes 4718592 | tf_op jit(solution)/shard_map/all_gather | solution.py:194
  74.3 396.0 %reduce-scatter.5.cloned.1.call-start = ((), (), s32[]{:S(2)}) async-start(), calls=%async_computation.13 | async-start | bytes 4718592 | tf_op jit(solution)/shard_map/reduce_scatter | solution.py:197
  84.2 14.7 %copy-start.4 = (bf16[1024,2048]{1,0:T(8,128)(2,1)S(1)}, bf16[1024,2048]{1,0:T(8,128)(2,1)}, u32[]{:S(2)}) copy-start(bf16[1024,2048]{1,0:T(8,128)(2,1)} %all-gather.3.cloned.1.call-done) | copy-start | bytes 12582916
  84.2 14.7 %copy-start.7 = (pred[2048,1792]{1,0:T(32,128)(4,1)S(1)}, pred[2048,1792]{1,0:T(32,128)(4,1)}, u32[]{:S(2)}) copy-start(pred[2048,1792]{1,0:T(32,128)(4,1)} %fusion.3) | copy-start | bytes 11010052
  116.3 14.4 %copy-start = (bf16[1792,1024]{0,1:T(8,128)(2,1)S(1)}, bf16[1792,1024]{0,1:T(8,128)(2,1)}, u32[]{:S(2)}) copy-start(bf16[1792,1024]{0,1:T(8,128)(2,1)} %convolution_convert_fusion.3) | copy-start | bytes 11010052
  130.6 278.2 %slice-start = ((s8[7340032]{0:T(1024)(128)(4,1)}), s8[3145728]{0:T(1024)(128)(4,1)S(1)}, s32[]{:S(2)}) async-start(s8[7340032]{0:T(1024)(128)(4,1)} %bitcast.73), calls=%async_computation.14 | async-start | bytes 6291456
  399.8 9.0 %slice-start.1 = ((s8[7340032]{0:T(1024)(128)(4,1)}), s8[4194304]{0:T(1024)(128)(4,1)S(1)}, s32[]{:S(2)}) async-start(s8[7340032]{0:T(1024)(128)(4,1)} %bitcast.73), calls=%async_computation.15 | async-start | bytes 8388608
  399.8 10.5 %copy-start.6 = (pred[1792,2048]{1,0:T(32,128)(4,1)S(1)}, pred[1792,2048]{1,0:T(32,128)(4,1)}, u32[]{:S(2)}) copy-start(pred[1792,2048]{1,0:T(32,128)(4,1)} %fusion.2) | copy-start | bytes 11010052
  406.9 1.9 copy-start.2
  419.7 14.3 %slice-start.2 = ((s8[7340032]{0:T(1024)(128)(4,1)}), s8[3145728]{0:T(1024)(128)(4,1)S(1)}, s32[]{:S(2)}) async-start(s8[7340032]{0:T(1024)(128)(4,1)} %bitcast.75), calls=%async_computation.16 | async-start | bytes 6291456
  419.7 110.3 %reduce-scatter.3.cloned.1.call-start = ((), (), s32[]{:S(2)}) async-start(), calls=%async_computation.12 | async-start | bytes 4718592 | tf_op jit(solution)/shard_map/reduce_scatter | solution.py:197
  419.7 14.2 %copy-start.1 = (bf16[1,64,16,1792]{3,2,1,0:T(8,128)(2,1)S(1)}, bf16[1,64,16,1792]{3,2,1,0:T(8,128)(2,1)}, u32[]{:S(2)}) copy-start(bf16[1,64,16,1792]{3,2,1,0:T(8,128)(2,1)} %get-tuple-element.14) | copy-start | bytes 11010052
  419.8 14.2 %slice-start.3 = ((s8[7340032]{0:T(1024)(128)(4,1)}), s8[4194304]{0:T(1024)(128)(4,1)S(1)}, s32[]{:S(2)}) async-start(s8[7340032]{0:T(1024)(128)(4,1)} %bitcast.75), calls=%async_computation.17 | async-start | bytes 8388608
  419.8 14.2 %copy-start.8 = (pred[2048,1792]{1,0:T(32,128)(4,1)S(1)}, pred[2048,1792]{1,0:T(32,128)(4,1)}, u32[]{:S(2)}) copy-start(pred[2048,1792]{1,0:T(32,128)(4,1)} %fusion.3) | copy-start | bytes 11010052
  470.2 19.1 %all-to-all-start.4 = ((bf16[4,32,2048]{2,1,0:T(8,128)(2,1)}), bf16[4,32,2048]{2,1,0:T(8,128)(2,1)S(1)}, u32[]{:S(2)}, u32[]{:S(2)}) async-start(bf16[4,32,2048]{2,1,0:T(8,128)(2,1)} %bitcast.72), calls=%async_computation.6 | async-start | bytes 1048576 | tf_op jit(solution)/shard_map/all_to_all | solution.py:200
  491.0 39.0 %all-to-all-start.5 = ((bf16[32,8,1024]{2,0,1:T(8,128)(2,1)}), bf16[32,8,1024]{2,0,1:T(8,128)(2,1)S(1)}, u32[]{:S(2)}, u32[]{:S(2)}) async-start(bf16[32,8,1024]{2,0,1:T(8,128)(2,1)} %copy.36), calls=%async_computation.7 | async-start | bytes 1048576 | tf_op jit(solution)/shard_map/all_to_all | solution.py:201
  550.7 16.9 %all-to-all-start.7 = ((bf16[32,8,1024]{2,0,1:T(8,128)(2,1)}), bf16[32,8,1024]{2,0,1:T(8,128)(2,1)S(1)}, u32[]{:S(2)}, u32[]{:S(2)}) async-start(bf16[32,8,1024]{2,0,1:T(8,128)(2,1)} %copy.39), calls=%async_computation.9 | async-start | bytes 1048576 | tf_op jit(solution)/shard_map/all_to_all | solution.py:201
Sparse Core Ops, SparseCore 0:
  42.0 35.5 all-gather.2
  79.5 36.6 all-gather.4
  419.8 50.3 reduce-scatter.4
  474.4 55.5 reduce-scatter.2
